TPU v7x, 256 devices: a whole 4x4x8 slice. The times are simulated.
256 devices in a mesh: blk: 64 (over z, y, core), lag: 4 (over x).
Axes of the slice: x: 4, y: 4, z: 8, core: 2. Of those that a mesh axis runs over, the one named last changes fastest.
Arguments:
- excitation: bfloat16 [2, 65536, 128], P(None, 'blk'), may hold values from -6 to 6
- history: bfloat16 [16, 65536, 128], P('lag', 'blk'), may hold values from -6 to 6
- inter: bfloat16 [16, 64, 16, 4, 128, 128], P('lag', 'blk'), may hold values from -0.046875 to 0.046875
- src_lists: int32 [16, 64, 16, 4], P('lag', 'blk'), may hold values from 0 to 7, as said below
- dest_blocks: int32 [16, 64, 16], P('lag', 'blk'), may hold values from 0 to 511, as said below
- near: bfloat16 [512, 8, 128, 128], P('blk'), may hold values from -0.09375 to 0.09375
- diag_inverse: bfloat16 [512, 128, 128], P('blk'), may hold values from -0.5 to 0.5
- nbr_ids: int32 [512, 8], P('blk'), may hold values from 0 to 511, as said below
Outputs:
- currents: bfloat16 [2, 65536, 128], P(None, 'blk')
Inputs may be any that keep to these rules, and one draw needn't show every extreme that they name: `dest_blocks`: for each source device and each group of 4 lags starting at a multiple of 4, at most 2 of its 64 entries lie on any one device (the two may name the same block), and exactly 2 entries lie on one device. `src_lists`: the 4 entries of one slot are distinct. `nbr_ids`: the 8 entries of a block are distinct, differ from the block itself, and lie on the block's device or one of the two beside it along blk.
All inputs are finite; a program needn't handle non-finite values.
Results may differ from a plain program's by a relative error of at most 0.019.
Values may be sent and summed in bfloat16 or wider, within the bound.
No kernel may reach another device: no remote copies, remote signals or barrier semaphores. Data moves between devices by JAX's collectives and lax.ppermute only.
A program may use at most 128 MiB of HBM per device.

v0:
```python
import functools

import jax
import jax.numpy as jnp
from jax import lax
from jax.experimental import pallas as pl
from jax.experimental.pallas import tpu as pltpu
from jax.sharding import Mesh, PartitionSpec as P

SWEEPS = 3
NZ, NY, NC, NX = 8, 4, 2, 4
BLKS = 8
B = 128
RW = 32
BF = jnp.bfloat16
F32 = jnp.float32
VM = pl.BlockSpec(memory_space=pltpu.VMEM)
SM = pl.BlockSpec(memory_space=pltpu.SMEM)
ANY = pl.BlockSpec(memory_space=pl.ANY)
HBM = pl.BlockSpec(memory_space=pltpu.HBM)
BLK = ("z", "y", "c")


def shape(*dims, dtype=BF):
    return jax.ShapeDtypeStruct(dims, dtype)


def cost(flops, bytes_accessed):
    return pl.CostEstimate(flops=int(flops), bytes_accessed=int(bytes_accessed), transcendentals=0)


def params(mib=24):
    return pltpu.CompilerParams(vmem_limit_bytes=mib * 1024 * 1024)


def shift(value, axis, distance):
    count = lax.axis_size(axis)
    return lax.ppermute(value, axis, [(i, (i + distance) % count) for i in range(count)])


def parcels_kernel(first_ref, src_ref, past_ref, inter_ref, *rest):
    outs, held = rest[:-1], rest[-1]
    k = pl.program_id(0)
    for j in range(16):
        total = None
        for i in range(4):
            source = src_ref[k, 0, j, i]
            term = jnp.dot(inter_ref[0, j, i], past_ref[0, source], preferred_element_type=F32)
            total = term if total is None else total + term
        turned = total.T.astype(BF)
        if len(outs) == 1:
            for n in range(NX):
                outs[0][n, j] = turned[n * RW : (n + 1) * RW]
        else:
            held[j] = turned
    if len(outs) > 1:
        for distance in range(NX):
            start = pl.multiple_of(lax.rem(first_ref[0] + distance, NX) * RW, RW)
            outs[distance][...] = held[:, pl.ds(start, RW), :]


def parcels(first, sources, past, coupling, apart):
    whole = (pl.BlockSpec((NX, 16, RW, B), lambda k: (0, k, 0, 0)), shape(NX, 64, RW, B))
    part = (pl.BlockSpec((16, RW, B), lambda k: (k, 0, 0)), shape(64, RW, B))
    outs = [part] * NX if apart else [whole]
    return pl.pallas_call(
        parcels_kernel,
        grid=(4,),
        in_specs=[
            SM,
            SM,
            pl.BlockSpec((1, BLKS, B, B), lambda k: (k, 0, 0, 0)),
            pl.BlockSpec((1, 16, 4, B, B), lambda k: (k, 0, 0, 0, 0)),
        ],
        out_specs=[spec for spec, _ in outs],
        out_shape=[dims for _, dims in outs],
        scratch_shapes=[pltpu.VMEM((16, B, B), BF)],
        compiler_params=params(60),
        cost_estimate=cost(1, 1),
    )(first, sources, past, coupling)


def place_kernel(per, places_ref, *rest):
    ins, (out_ref, dense, sem) = rest[:-3], rest[-3:]
    dense[...] = jnp.zeros_like(dense)
    for n, values in enumerate(ins):

        def body(p, carry, n=n, values=values):
            at = places_ref[n * per + p]
            dense[at] = dense[at] + values[p]
            return carry

        lax.fori_loop(0, per, body, 0, unroll=8)
    copy = pltpu.make_async_copy(dense.at[pl.ds(0, 256)], out_ref, sem)
    copy.start()
    copy.wait()


def place(places, buffers):
    return pl.pallas_call(
        functools.partial(place_kernel, buffers[0].shape[0]),
        in_specs=[SM] + [VM] * len(buffers),
        out_specs=HBM,
        out_shape=shape(256, RW, B),
        scratch_shapes=[pltpu.VMEM((257, RW, B), BF), pltpu.SemaphoreType.DMA],
        compiler_params=params(),
        cost_estimate=cost(1, 1),
    )(places, *buffers)


def add_kernel(halves, out_ref):
    for n in range(NZ):
        total = halves[pl.ds(n * BLKS, BLKS)].astype(F32)
        for m in range(1, NY):
            total = total + halves[pl.ds(m * 64 + n * BLKS, BLKS)].astype(F32)
        out_ref[pl.ds(n * BLKS, BLKS)] = total.astype(BF)


def add(halves):
    return pl.pallas_call(
        add_kernel,
        in_specs=[VM],
        out_specs=VM,
        out_shape=shape(64, RW, B),
        compiler_params=params(),
        cost_estimate=cost(1, 1),
    )(halves)


def add_late_kernel(y_ref, places_ref, dense_ref, *rest):
    others, late, (out_ref, total, own, sem) = rest[:3], rest[3:5], rest[5:]
    start = pl.multiple_of(y_ref[0] * 64, 64)
    copy = pltpu.make_async_copy(dense_ref.at[pl.ds(start, 64)], own, sem)
    copy.start()
    for n in range(NZ):
        part = pl.ds(n * BLKS, BLKS)
        total[part] = sum(value[part].astype(F32) for value in others)
    copy.wait()
    for n in range(NZ):
        part = pl.ds(n * BLKS, BLKS)
        total[part] = total[part] + own[part].astype(F32)
    for n in range(2):

        def body(p, carry, n=n):
            at = places_ref[n * 64 + p]

            @pl.when(at < 64)
            def _():
                total[at] = total[at] + late[n][p].astype(F32)

            return carry

        lax.fori_loop(0, 64, body, 0, unroll=8)
    for n in range(NZ):
        part = pl.ds(n * BLKS, BLKS)
        out_ref[part] = total[part].astype(BF)


def add_late(y, places, dense, others, late):
    return pl.pallas_call(
        add_late_kernel,
        in_specs=[SM, SM, ANY] + [VM] * 5,
        out_specs=VM,
        out_shape=shape(64, RW, B),
        scratch_shapes=[
            pltpu.VMEM((64, RW, B), F32),
            pltpu.VMEM((64, RW, B), BF),
            pltpu.SemaphoreType.DMA,
        ],
        compiler_params=params(),
        cost_estimate=cost(1, 1),
    )(y, places, dense, *others, *late)


def total_of(ref, count):
    total = ref[pl.ds(0, BLKS)].astype(F32)
    for n in range(1, count):
        total = total + ref[pl.ds(n * BLKS, BLKS)].astype(F32)
    return total


def first_solve_kernel(pieces, incident, inverse, drive_ref, current_ref):
    drive = incident[...].astype(F32) - total_of(pieces, NZ)
    drive_ref[...] = drive
    rounded = drive.astype(BF)
    for g in range(BLKS):
        current_ref[g] = jnp.dot(rounded[g], inverse[g], preferred_element_type=F32).astype(BF)


def first_solve(pieces, incident, inverse):
    return pl.pallas_call(
        first_solve_kernel,
        in_specs=[VM] * 3,
        out_specs=[VM] * 2,
        out_shape=[shape(BLKS, RW, B, dtype=F32), shape(BLKS, RW, B)],
        compiler_params=params(),
        cost_estimate=cost(1, 1),
    )(pieces, incident, inverse)


def sweep_kernel(ids_ref, right, own, left, drive_ref, near_ref, inverse, out_ref, held):
    held[0:BLKS] = left[...]
    held[BLKS : 2 * BLKS] = own[...]
    held[2 * BLKS : 3 * BLKS] = right[...]
    for g in range(BLKS):
        gathered = jnp.concatenate([held[ids_ref[g * 8 + m]] for m in range(8)], axis=1)
        pull = jnp.dot(gathered, near_ref[g], preferred_element_type=F32)
        rest = (drive_ref[g] - pull).astype(BF)
        out_ref[g] = jnp.dot(rest, inverse[g], preferred_element_type=F32).astype(BF)


def sweep(ids, right, own, left, drive, near, inverse):
    return pl.pallas_call(
        sweep_kernel,
        in_specs=[SM] + [VM] * 6,
        out_specs=VM,
        out_shape=shape(BLKS, RW, B),
        scratch_shapes=[pltpu.VMEM((3 * BLKS, RW, B), BF)],
        compiler_params=params(),
        cost_estimate=cost(1, 1),
    )(ids, right, own, left, drive, near, inverse)


def late_parcels_kernel(x_ref, src_ref, current, *rest):
    (own, low, high, *far), (out_ref, coupling, sem) = rest[:5], rest[5:]
    x = x_ref[0]
    for half in range(2):
        part = pl.ds(half * 8, 8)
        choices = (own.at[part], low.at[part], far[half], high.at[part])
        for who, source in enumerate(choices):

            @pl.when(x == who)
            def _(part=part, half=half, source=source):
                pltpu.make_async_copy(source, coupling.at[part], sem.at[half]).start()

    for half in range(2):
        part = coupling.at[pl.ds(half * 8, 8)]
        pltpu.make_async_copy(part, part, sem.at[half]).wait()
        for j in range(half * 8, half * 8 + 8):
            gathered = jnp.concatenate([current[src_ref[j * 4 + i]] for i in range(4)], axis=1)
            parcel = jnp.dot(gathered, coupling[j], preferred_element_type=F32).astype(BF)
            for copy in range(NY):
                out_ref[copy * 16 + j] = parcel


def late_parcels(x, sources, current, couplings):
    return pl.pallas_call(
        late_parcels_kernel,
        in_specs=[SM, SM, VM] + [ANY] * 5,
        out_specs=VM,
        out_shape=shape(NY * 16, RW, B),
        scratch_shapes=[pltpu.VMEM((16, 4 * B, B), BF), pltpu.SemaphoreType.DMA((2,))],
        compiler_params=params(),
        cost_estimate=cost(1, 1),
    )(x, sources, current, *couplings)


def finish_kernel(x_ref, *refs):
    ins, out_ref, held = refs[:8], refs[8], refs[9]
    for step in range(2):
        for distance in range(4):
            start = pl.multiple_of(lax.rem(x_ref[0] + NX - distance, NX) * RW, RW)
            held[:, pl.ds(start, RW), :] = ins[step * 4 + distance][...]
        for g in range(BLKS):
            out_ref[step, g] = held[g].T


def finish(x, pieces):
    return pl.pallas_call(
        finish_kernel,
        in_specs=[SM] + [VM] * 8,
        out_specs=VM,
        out_shape=shape(2, BLKS, B, B),
        scratch_shapes=[pltpu.VMEM((BLKS, B, B), BF)],
        compiler_params=params(),
        cost_estimate=cost(1, 1),
    )(x, *pieces)


def spread(value, axis):
    return [value, shift(value, axis, 1), shift(value, axis, 2), shift(value, axis, -1)]


def after(value, *others):
    return lax.optimization_barrier((value,) + others)[0]


def exchange(value, axis):
    return lax.all_to_all(value, axis, split_axis=0, concat_axis=0, tiled=True)


def per_device(excitation, history, inter, src_lists, dest_blocks, near, diag_inverse, nbr_ids):
    x, y, z, c = (lax.axis_index(name) for name in ("x", "y", "z", "c"))
    position = (z * NY + y) * NC + c
    x_scalar = x.astype(jnp.int32).reshape(1)
    past = history.reshape(4, BLKS, B, B)
    coupling = inter[:, 0]

    meta = jnp.concatenate([dest_blocks[:, 0].reshape(64), src_lists[0, 0].reshape(64)])
    metas = exchange(jnp.broadcast_to(meta[None], (NX, 128)), "x")

    older = lax.ppermute(past[3], "x", [(i, i + 1) for i in range(NX - 1)])
    (sent,) = parcels(x_scalar, src_lists, past, coupling, False)
    sent = after(sent, older, metas)
    crossed = exchange(sent, "x")
    later_past = jnp.concatenate([after(older, sent)[None], past[:3]], 0)
    later_sent = parcels(x_scalar, src_lists, later_past, coupling, True)

    metas = after(metas, sent)
    metas = jnp.stack([metas, shift(metas, "c", 1)])
    late_sources = metas[0, 0, 64:]
    targets = metas[:, :, :64]
    late_targets = jnp.stack(spread(metas[:, 0, :16], "y"), axis=1)
    late_targets = jnp.take(late_targets, (y - jnp.arange(NY)) % NY, axis=1)

    def place_of(target):
        device = target // BLKS
        inner = device // NC // NY * BLKS + target % BLKS
        return device % NC == c, device // NC % NY, inner

    same, across, inner = place_of(targets)
    places = jnp.where(same, across * 64 + inner, 256).reshape(512)
    same, across, inner = place_of(late_targets)
    late_places = jnp.where(same & (across == y), inner, 64).reshape(128)

    by_distance = places.reshape(2, NX, 64)[:, (x - jnp.arange(NX)) % NX].reshape(512)
    newest = after(coupling[0], sent).swapaxes(2, 3).reshape(16, 4 * B, B)
    crossed = after(crossed, later_sent, places, by_distance, late_places, newest)
    crossed = crossed.reshape(256, RW, B)
    dense = place(places, [crossed, shift(crossed, "c", 1)])
    halves = exchange(dense, "y")
    later_sent = after(later_sent, dense)
    steps = (0, 1, 2, -1)
    later_crossed = [later_sent[0]] + [
        shift(later_sent[n], "x", steps[n]) for n in range(1, NX)
    ]

    near, diag_inverse, excitation = after((near, diag_inverse, excitation), dense)
    near_t = near.swapaxes(2, 3).reshape(BLKS, 8 * B, B)
    inverse_t = diag_inverse.swapaxes(1, 2)
    incident = excitation.reshape(2, BLKS, B, B).swapaxes(2, 3)
    incident = lax.dynamic_slice_in_dim(incident, x * RW, RW, axis=2)
    ids = (nbr_ids - (position - 1) * BLKS).reshape(64)

    def one_sweep(current, drive):
        ends = NZ * NY * NC - 1
        right = lax.ppermute(current, BLK, [(i + 1, i) for i in range(ends)])
        left = lax.ppermute(current, BLK, [(i, i + 1) for i in range(ends)])
        return sweep(ids, right, current, left, drive, near_t, inverse_t)

    later_own = shift(later_crossed[0], "c", 1)
    later_crossed = after(later_crossed, near_t, inverse_t, incident, ids, later_own)

    start = after(newest, later_crossed)
    low = lax.ppermute(start, "x", [(0, 1)])
    high = lax.ppermute(start, "x", [(0, 3)])
    halves = after(halves, later_crossed, later_own, near_t, inverse_t, incident, ids)
    summed = add(halves)
    pieces = exchange(summed, "z")

    later_other = [later_own] + [shift(value, "c", 1) for value in later_crossed[1:]]
    later_dense = place(by_distance, later_crossed + later_other)

    def other_part(distance):
        start = (y + distance) % NY * 64
        return lax.dynamic_slice_in_dim(later_dense, start, 64, axis=0)

    parts = [other_part(n) for n in range(1, NY)]
    pieces = after(pieces, later_dense, parts)
    later_halves = [shift(parts[n], "y", steps[n + 1]) for n in range(3)]

    drive, current = first_solve(pieces, incident[0], inverse_t)
    current = one_sweep(current, drive)
    current = after(current, later_halves[0], later_halves[2])
    current = one_sweep(current, drive)
    current, low, high = after((current, low, high), later_halves[1])
    far = [lax.ppermute(low[:8], "x", [(1, 2)]), lax.ppermute(high[8:], "x", [(3, 2)])]
    current = one_sweep(current, drive)
    outputs = spread(current, "x")

    couplings = after([newest, low, high] + far, current)
    late = exchange(late_parcels(x_scalar, late_sources, current, couplings), "y")
    y_scalar = y.astype(jnp.int32).reshape(1)
    late = [late, shift(late, "c", 1)]
    pieces = exchange(add_late(y_scalar, late_places, later_dense, later_halves, late), "z")
    pieces = after(pieces, outputs)
    drive, current = first_solve(pieces, incident[1], inverse_t)
    for _ in range(SWEEPS):
        current = one_sweep(current, drive)
    outputs = outputs + spread(current, "x")
    return finish(x_scalar, outputs).reshape(2, BLKS * B, B)


def solution(mesh):
    grid = Mesh(mesh.devices.reshape(NZ, NY, NC, NX), ("z", "y", "c", "x"))
    placed = (
        P(None, BLK, None),
        P("x", BLK, None),
        P("x", BLK, None, None, None, None),
        P("x", BLK, None, None),
        P("x", BLK, None),
        P(BLK, None, None, None),
        P(BLK, None, None),
        P(BLK, None),
    )
    return jax.shard_map(
        per_device, mesh=grid, in_specs=placed, out_specs=P(None, BLK, None), check_vma=False
    )
```

profile of v0, /device:TPU:121, one launch (start us, length us, event | category | flops | bytes accessed | tf_op | source)
XLA Modules:
  0.0 279.0 jit_solution(11135142126170742205)
XLA Ops:
  1.0 3.1 %collective-permute-start = (bf16[8,128,128]{2,1,0:T(8,128)(2,1)S(1)}, bf16[8,128,128]{2,1,0:T(8,128)(2,1)S(1)}, u32[]{:S(2)}, u32[]{:S(2)}) collective-permute-start(bf16[8,128,128]{2,1,0:T(8,128)(2,1)S(1)} %bitcast.69), channel_id=1, source_target_pairs={{0,1},{1,2},{2,3},{4,5},{5,6},{6,7},{8,9},{9,10},{10,11},{12,13},{... | collective-permute-start | bytes 786440 | tf_op jit(solution)/shard_map/ppermute | solution.py:302
  7.6 3.7 %all-to-all-start = ((s32[4,1,128]{2,1,0:T(1,128)}), s32[4,1,128]{2,1,0:T(1,128)S(1)}, u32[]{:S(2)}, u32[]{:S(2)}) async-start(s32[4,1,128]{2,1,0:T(1,128)} %broadcast_in_dim.28), calls=%async_computation | async-start | bytes 4096 | tf_op jit(solution)/shard_map/all_to_all | solution.py:289
  12.8 7.0 %shard_map.82 = bf16[4,64,32,128]{3,2,1,0:T(8,128)(2,1)} custom-call(s32[1]{0:T(128)} %bitcast.first_ref.x_ref, s32[4,1,16,4]{3,2,1,0:T(8,128)} %copy.29.src_ref, bf16[4,8,128,128]{3,2,1,0:T(8,128)(2,1)} %bitcast.65, bf16[4,16,4,128,128]{4,3,2,1,0:T(8,128)(2,1)} %bitcast.62), custom_call_target="tpu_custom_call" | custom-call | flops 1 | bytes 1 | tf_op jit(solution)/shard_map/pallas_call | solution.py:66
  20.8 4.2 %all-to-all-start.1 = ((bf16[4,64,32,128]{3,2,1,0:T(8,128)(2,1)}), bf16[4,64,32,128]{3,2,1,0:T(8,128)(2,1)S(1)}, u32[]{:S(2)}, u32[]{:S(2)}) async-start(bf16[4,64,32,128]{3,2,1,0:T(8,128)(2,1)} %shard_map.82), calls=%async_computation.1 | async-start | bytes 4194304 | tf_op jit(solution)/shard_map/all_to_all | solution.py:289
  25.1 3.3 %slice_bitcast_fusion = bf16[16,4,128,128]{3,2,1,0:T(8,128)(2,1)} fusion(bf16[4,1,16,4,128,128]{5,4,3,2,1,0:T(8,128)(2,1)} %param.10), kind=kLoop, calls=%fused_computation.2 | loop fusion | bytes 4194304 | tf_op jit(solution)/shard_map/squeeze | solution.py:327
  31.3 7.0 %shard_map.83 = (bf16[64,32,128]{2,1,0:T(8,128)(2,1)}, bf16[64,32,128]{2,1,0:T(8,128)(2,1)}, bf16[64,32,128]{2,1,0:T(8,128)(2,1)}, bf16[64,32,128]{2,1,0:T(8,128)(2,1)}) custom-call(s32[1]{0:T(128)} %bitcast.first_ref.x_ref, s32[4,1,16,4]{3,2,1,0:T(8,128)} %copy.29.src_ref, bf16[4,8,128,128]{3,2,1,0:T(8,128)(2,1)} %pad_maximum_fusion.past_ref, ...), custom_call_target="tpu_custom_call" | custom-call | flops 1 | bytes 1 | tf_op jit(solution)/shard_map/pallas_call | solution.py:66
  38.3 3.9 %copy.35 = bf16[16,4,128,128]{3,2,1,0:T(8,128)(2,1)} copy(bf16[16,4,128,128]{2,3,1,0:T(8,128)(2,1)} %bitcast.64) | data formatting | bytes 4194304 | tf_op jit(solution)/shard_map/transpose | solution.py:327
  49.6 2.7 collective-permute-start.5
  52.3 3.8 %collective-permute-done.5.rest_1_ = bf16[256,32,128]{2,1,0:T(8,128)(2,1)S(1)} collective-permute-done((bf16[256,32,128]{2,1,0:T(8,128)(2,1)S(1)}, bf16[256,32,128]{2,1,0:T(8,128)(2,1)S(1)}, u32[]{:S(2)}, u32[]{:S(2)}) %collective-permute-start.5) | collective-permute-done | bytes 2097184 | tf_op jit(solution)/shard_map/ppermute | solution.py:38
  56.1 3.7 %shard_map.84 = bf16[256,32,128]{2,1,0:T(8,128)(2,1)S(1)} custom-call(s32[512]{0:T(512)S(1)} %reshape.155.places_ref, bf16[256,32,128]{2,1,0:T(8,128)(2,1)S(1)} %bitcast.61, bf16[256,32,128]{2,1,0:T(8,128)(2,1)S(1)} %collective-permute-done.5.rest_1_), custom_call_target="tpu_custom_call" | custom-call | flops 1 | bytes 1 | tf_op jit(solution)/shard_map/pallas_call | solution.py:100
  61.2 4.6 %all-to-all-start.2 = ((bf16[256,32,128]{2,1,0:T(8,128)(2,1)}), bf16[256,32,128]{2,1,0:T(8,128)(2,1)}, u32[]{:S(2)}, u32[]{:S(2)}) async-start(bf16[256,32,128]{2,1,0:T(8,128)(2,1)} %copy-done.4), calls=%async_computation.2 | async-start | bytes 4194304 | tf_op jit(solution)/shard_map/all_to_all | solution.py:289
  66.7 2.4 collective-permute-start.7
  73.2 3.0 %copy.36 = bf16[8,8,128,128]{3,2,1,0:T(8,128)(2,1)S(1)} copy(bf16[8,8,128,128]{2,3,1,0:T(8,128)(2,1)} %bitcast.67) | data formatting | bytes 4194304 | tf_op jit(solution)/shard_map/transpose | solution.py:339
  76.2 4.0 %collective-permute-done.6.rest_1_ = bf16[64,32,128]{2,1,0:T(8,128)(2,1)} collective-permute-done((bf16[64,32,128]{2,1,0:T(8,128)(2,1)}, bf16[64,32,128]{2,1,0:T(8,128)(2,1)}, u32[]{:S(2)}, u32[]{:S(2)}) %collective-permute-start.6) | collective-permute-done | bytes 524320 | tf_op jit(solution)/shard_map/ppermute | solution.py:38
  80.2 11.8 %collective-permute-done.7.rest_2_ = bf16[64,32,128]{2,1,0:T(8,128)(2,1)} collective-permute-done((bf16[64,32,128]{2,1,0:T(8,128)(2,1)}, bf16[64,32,128]{2,1,0:T(8,128)(2,1)}, u32[]{:S(2)}, u32[]{:S(2)}) %collective-permute-start.7) | collective-permute-done | bytes 524320 | tf_op jit(solution)/shard_map/ppermute | solution.py:38
  92.0 6.7 %collective-permute-start.20 = (bf16[16,512,128]{2,1,0:T(8,128)(2,1)}, bf16[16,512,128]{2,1,0:T(8,128)(2,1)}, u32[]{:S(2)}, u32[]{:S(2)}) collective-permute-start(bf16[16,512,128]{2,1,0:T(8,128)(2,1)} %bitcast.57), channel_id=1, source_target_pairs={{0,3},{4,7},{8,11},{12,15},{16,19},{20,23},{24,27},{28,31},{32,35}... | collective-permute-start | bytes 6291464 | tf_op jit(solution)/shard_map/ppermute | solution.py:356
  98.7 2.6 collective-permute-start.19
  101.3 2.6 shard_map.85
  104.0 7.1 %all-to-all-start.3 = ((bf16[64,32,128]{2,1,0:T(8,128)(2,1)}), bf16[64,32,128]{2,1,0:T(8,128)(2,1)S(1)}, u32[]{:S(2)}, u32[]{:S(2)}) async-start(bf16[64,32,128]{2,1,0:T(8,128)(2,1)} %shard_map.85), calls=%async_computation.3 | async-start | bytes 1048576 | tf_op jit(solution)/shard_map/all_to_all | solution.py:289
  116.8 5.1 %shard_map.86.dense_ref = bf16[256,32,128]{2,1,0:T(8,128)(2,1)S(1)} custom-call(s32[512]{0:T(512)S(1)} %reshape.156.places_ref, bf16[64,32,128]{2,1,0:T(8,128)(2,1)S(1)} %copy-done.7, bf16[64,32,128]{2,1,0:T(8,128)(2,1)} %collective-permute-done.6.rest_1_, bf16[64,32,128]{2,1,0:T(8,128)(2,1)} %collective-permute-done.7.rest_2_, ...), custom_call_target="tpu_custom_call" | custom-call | flops 1 | bytes 1 | tf_op jit(solution)/shard_map/pallas_call | solution.py:100
  124.8 4.3 %collective-permute-start.14 = (bf16[8,32,128]{2,1,0:T(8,128)(2,1)S(1)}, bf16[8,32,128]{2,1,0:T(8,128)(2,1)S(1)}, u32[]{:S(2)}, u32[]{:S(2)}) collective-permute-start(bf16[8,32,128]{2,1,0:T(8,128)(2,1)S(1)} %get-tuple-element.64.own), channel_id=1, source_target_pairs={{0,4},{4,8},{8,12},{12,16},{16,20},{20,24},{24,28},{28,32},{32,36}... | collective-permute-start | bytes 196616 | tf_op jit(solution)/shard_map/ppermute | solution.py:348
  129.4 2.4 collective-permute-start.15
  133.7 7.1 %collective-permute-done.13.right = bf16[8,32,128]{2,1,0:T(8,128)(2,1)S(1)} collective-permute-done((bf16[8,32,128]{2,1,0:T(8,128)(2,1)S(1)}, bf16[8,32,128]{2,1,0:T(8,128)(2,1)S(1)}, u32[]{:S(2)}, u32[]{:S(2)}) %collective-permute-start.13) | collective-permute-done | bytes 65568 | tf_op jit(solution)/shard_map/ppermute | solution.py:347
  140.8 3.6 %collective-permute-start.21 = (bf16[64,32,128]{2,1,0:T(8,128)(2,1)}, bf16[64,32,128]{2,1,0:T(8,128)(2,1)S(1)}, u32[]{:S(2)}, u32[]{:S(2)}) collective-permute-start(bf16[64,32,128]{2,1,0:T(8,128)(2,1)} %get-tuple-element.80), channel_id=1, source_target_pairs={{0,16},{8,24},{16,0},{24,8},{1,17},{9,25},{17,1},{25,9},{2,18},{10... | collective-permute-start | bytes 1572872 | tf_op jit(solution)/shard_map/ppermute | solution.py:38
  146.4 8.4 %collective-permute-done.15.rest_0_ = bf16[64,32,128]{2,1,0:T(8,128)(2,1)S(1)} collective-permute-done((bf16[64,32,128]{2,1,0:T(8,128)(2,1)}, bf16[64,32,128]{2,1,0:T(8,128)(2,1)S(1)}, u32[]{:S(2)}, u32[]{:S(2)}) %collective-permute-start.15) | collective-permute-done | bytes 524320 | tf_op jit(solution)/shard_map/ppermute | solution.py:38
  156.7 2.4 collective-permute-start.17
  159.1 6.5 %collective-permute-done.17.right = bf16[8,32,128]{2,1,0:T(8,128)(2,1)S(1)} collective-permute-done((bf16[8,32,128]{2,1,0:T(8,128)(2,1)S(1)}, bf16[8,32,128]{2,1,0:T(8,128)(2,1)S(1)}, u32[]{:S(2)}, u32[]{:S(2)}) %collective-permute-start.17) | collective-permute-done | bytes 65568 | tf_op jit(solution)/shard_map/ppermute | solution.py:347
  165.6 1.9 shard_map.89.own
  173.7 2.4 collective-permute-start.22
  176.2 6.4 %collective-permute-done.22.right = bf16[8,32,128]{2,1,0:T(8,128)(2,1)S(1)} collective-permute-done((bf16[8,32,128]{2,1,0:T(8,128)(2,1)S(1)}, bf16[8,32,128]{2,1,0:T(8,128)(2,1)S(1)}, u32[]{:S(2)}, u32[]{:S(2)}) %collective-permute-start.22) | collective-permute-done | bytes 65568 | tf_op jit(solution)/shard_map/ppermute | solution.py:347
  182.6 1.9 shard_map.90.current.refs_0_
  185.9 12.0 %all_to_all.34.rest_3_ = bf16[64,32,128]{2,1,0:T(8,128)(2,1)S(1)} all-to-all(bf16[64,32,128]{2,1,0:T(8,128)(2,1)S(1)} %shard_map.91), channel_id=1, replica_groups=mesh['z'=8,'y'=4,'c'=2,'x'=4] {'y'}, dimensions={0} | all-to-all | bytes 1048576 | tf_op jit(solution)/shard_map/all_to_all | solution.py:289
  199.8 2.2 shard_map.92
  202.8 4.5 %all-to-all-start.5 = ((bf16[64,32,128]{2,1,0:T(8,128)(2,1)}), bf16[64,32,128]{2,1,0:T(8,128)(2,1)S(1)}, u32[]{:S(2)}, u32[]{:S(2)}) async-start(bf16[64,32,128]{2,1,0:T(8,128)(2,1)} %copy-done.5), calls=%async_computation.5 | async-start | bytes 1048576 | tf_op jit(solution)/shard_map/all_to_all | solution.py:289
  207.3 6.5 %collective-permute-start.26 = (bf16[8,32,128]{2,1,0:T(8,128)(2,1)S(1)}, bf16[8,32,128]{2,1,0:T(8,128)(2,1)S(1)}, u32[]{:S(2)}, u32[]{:S(2)}) collective-permute-start(bf16[8,32,128]{2,1,0:T(8,128)(2,1)S(1)} %shard_map.90.current.refs_0_), channel_id=1, source_target_pairs={{0,3},{1,0},{2,1},{3,2},{4,7},{5,4},{6,5},{7,6},{8,11},{9,8},{10,9... | collective-permute-start | bytes 196616 | tf_op jit(solution)/shard_map/ppermute | solution.py:38
  213.8 4.0 %collective-permute-start.25 = (bf16[8,32,128]{2,1,0:T(8,128)(2,1)S(1)}, bf16[8,32,128]{2,1,0:T(8,128)(2,1)S(1)}, u32[]{:S(2)}, u32[]{:S(2)}) collective-permute-start(bf16[8,32,128]{2,1,0:T(8,128)(2,1)S(1)} %shard_map.90.current.refs_0_), channel_id=1, source_target_pairs={{0,2},{1,3},{2,0},{3,1},{4,6},{5,7},{6,4},{7,5},{8,10},{9,11},{10,... | collective-permute-start | bytes 196616 | tf_op jit(solution)/shard_map/ppermute | solution.py:38
  223.0 8.3 %collective-permute-start.31 = (bf16[8,32,128]{2,1,0:T(8,128)(2,1)S(1)}, bf16[8,32,128]{2,1,0:T(8,128)(2,1)S(1)}, u32[]{:S(2)}, u32[]{:S(2)}) collective-permute-start(bf16[8,32,128]{2,1,0:T(8,128)(2,1)S(1)} %get-tuple-element.77.own), channel_id=1, source_target_pairs={{0,4},{4,8},{8,12},{12,16},{16,20},{20,24},{24,28},{28,32},{32,36}... | collective-permute-start | bytes 196616 | tf_op jit(solution)/shard_map/ppermute | solution.py:348
  231.4 1.9 collective-permute-start.30
  233.3 7.0 %collective-permute-done.30.right = bf16[8,32,128]{2,1,0:T(8,128)(2,1)S(1)} collective-permute-done((bf16[8,32,128]{2,1,0:T(8,128)(2,1)S(1)}, bf16[8,32,128]{2,1,0:T(8,128)(2,1)S(1)}, u32[]{:S(2)}, u32[]{:S(2)}) %collective-permute-start.30) | collective-permute-done | bytes 65568 | tf_op jit(solution)/shard_map/ppermute | solution.py:347
  240.3 1.9 shard_map.94.own
  242.2 2.1 collective-permute-start.33
  244.3 2.4 collective-permute-start.32
  246.7 6.5 %collective-permute-done.32.right = bf16[8,32,128]{2,1,0:T(8,128)(2,1)S(1)} collective-permute-done((bf16[8,32,128]{2,1,0:T(8,128)(2,1)S(1)}, bf16[8,32,128]{2,1,0:T(8,128)(2,1)S(1)}, u32[]{:S(2)}, u32[]{:S(2)}) %collective-permute-start.32) | collective-permute-done | bytes 65568 | tf_op jit(solution)/shard_map/ppermute | solution.py:347
  255.1 1.9 collective-permute-start.35
  257.0 2.6 collective-permute-start.34
  259.7 6.3 %collective-permute-done.34.right = bf16[8,32,128]{2,1,0:T(8,128)(2,1)S(1)} collective-permute-done((bf16[8,32,128]{2,1,0:T(8,128)(2,1)S(1)}, bf16[8,32,128]{2,1,0:T(8,128)(2,1)S(1)}, u32[]{:S(2)}, u32[]{:S(2)}) %collective-permute-start.34) | collective-permute-done | bytes 65568 | tf_op jit(solution)/shard_map/ppermute | solution.py:347
  269.6 4.0 %collective-permute-start.37 = (bf16[8,32,128]{2,1,0:T(8,128)(2,1)S(1)}, bf16[8,32,128]{2,1,0:T(8,128)(2,1)S(1)}, u32[]{:S(2)}, u32[]{:S(2)}) collective-permute-start(bf16[8,32,128]{2,1,0:T(8,128)(2,1)S(1)} %shard_map.96.refs_4_), channel_id=1, source_target_pairs={{0,2},{1,3},{2,0},{3,1},{4,6},{5,7},{6,4},{7,5},{8,10},{9,11},{10,... | collective-permute-start | bytes 196616 | tf_op jit(solution)/shard_map/ppermute | solution.py:38
  275.3 2.7 collective-permute-done.36.refs_5_
  (136 shorter events, 61.9 us)
Async XLA Ops:
  0.0 72.1 %copy-start = (bf16[2,1024,128]{2,1,0:T(8,128)(2,1)S(1)}, bf16[2,1024,128]{2,1,0:T(8,128)(2,1)}, u32[]{:S(2)}) copy-start(bf16[2,1024,128]{2,1,0:T(8,128)(2,1)} %param.8) | copy-start | bytes 1572868
  1.0 19.7 %collective-permute-start = (bf16[8,128,128]{2,1,0:T(8,128)(2,1)S(1)}, bf16[8,128,128]{2,1,0:T(8,128)(2,1)S(1)}, u32[]{:S(2)}, u32[]{:S(2)}) collective-permute-start(bf16[8,128,128]{2,1,0:T(8,128)(2,1)S(1)} %bitcast.69), channel_id=1, source_target_pairs={{0,1},{1,2},{2,3},{4,5},{5,6},{6,7},{8,9},{9,10},{10,11},{12,13},{... | collective-permute-start | bytes 786440 | tf_op jit(solution)/shard_map/ppermute | solution.py:302
  7.6 13.1 %all-to-all-start = ((s32[4,1,128]{2,1,0:T(1,128)}), s32[4,1,128]{2,1,0:T(1,128)S(1)}, u32[]{:S(2)}, u32[]{:S(2)}) async-start(s32[4,1,128]{2,1,0:T(1,128)} %broadcast_in_dim.28), calls=%async_computation | async-start | bytes 4096 | tf_op jit(solution)/shard_map/all_to_all | solution.py:289
  20.8 28.8 %all-to-all-start.1 = ((bf16[4,64,32,128]{3,2,1,0:T(8,128)(2,1)}), bf16[4,64,32,128]{3,2,1,0:T(8,128)(2,1)S(1)}, u32[]{:S(2)}, u32[]{:S(2)}) async-start(bf16[4,64,32,128]{3,2,1,0:T(8,128)(2,1)} %shard_map.82), calls=%async_computation.1 | async-start | bytes 4194304 | tf_op jit(solution)/shard_map/all_to_all | solution.py:289
  28.4 13.8 %collective-permute-start.1 = (s32[4,128]{1,0:T(4,128)S(1)}, s32[4,128]{1,0:T(4,128)S(1)}, u32[]{:S(2)}, u32[]{:S(2)}) collective-permute-start(s32[4,128]{1,0:T(4,128)S(1)} %bitcast.71), channel_id=1, source_target_pairs={{0,4},{4,0},{1,5},{5,1},{2,6},{6,2},{3,7},{7,3},{8,12},{12,8},{9,1... | collective-permute-start | bytes 6152 | tf_op jit(solution)/shard_map/ppermute | solution.py:38
  42.2 4.0 %collective-permute-start.4 = (s32[2,16]{1,0:T(2,128)S(1)}, s32[2,16]{1,0:T(2,128)S(1)}, u32[]{:S(2)}, u32[]{:S(2)}) collective-permute-start(s32[2,16]{1,0:T(2,128)S(1)} %bitcast.78), channel_id=1, source_target_pairs={{0,24},{8,0},{16,8},{24,16},{1,25},{9,1},{17,9},{25,17},{2,26},{10... | collective-permute-start | bytes 392 | tf_op jit(solution)/shard_map/ppermute | solution.py:38
  42.8 4.2 %collective-permute-start.3 = (s32[2,16]{1,0:T(2,128)S(1)}, s32[2,16]{1,0:T(2,128)S(1)}, u32[]{:S(2)}, u32[]{:S(2)}) collective-permute-start(s32[2,16]{1,0:T(2,128)S(1)} %bitcast.79), channel_id=1, source_target_pairs={{0,16},{8,24},{16,0},{24,8},{1,17},{9,25},{17,1},{25,9},{2,18},{10... | collective-permute-start | bytes 392 | tf_op jit(solution)/shard_map/ppermute | solution.py:38
  43.4 3.6 %collective-permute-start.2 = (s32[2,16]{1,0:T(2,128)S(1)}, s32[2,16]{1,0:T(2,128)S(1)}, u32[]{:S(2)}, u32[]{:S(2)}) collective-permute-start(s32[2,16]{1,0:T(2,128)S(1)} %bitcast.80), channel_id=1, source_target_pairs={{0,8},{8,16},{16,24},{24,0},{1,9},{9,17},{17,25},{25,1},{2,10},{10... | collective-permute-start | bytes 392 | tf_op jit(solution)/shard_map/ppermute | solution.py:38
  49.6 6.5 %collective-permute-start.5 = (bf16[256,32,128]{2,1,0:T(8,128)(2,1)S(1)}, bf16[256,32,128]{2,1,0:T(8,128)(2,1)S(1)}, u32[]{:S(2)}, u32[]{:S(2)}) collective-permute-start(bf16[256,32,128]{2,1,0:T(8,128)(2,1)S(1)} %bitcast.60), channel_id=1, source_target_pairs={{0,4},{4,0},{1,5},{5,1},{2,6},{6,2},{3,7},{7,3},{8,12},{12,8},{9,1... | collective-permute-start | bytes 6291464 | tf_op jit(solution)/shard_map/ppermute | solution.py:38
  61.2 40.1 %all-to-all-start.2 = ((bf16[256,32,128]{2,1,0:T(8,128)(2,1)}), bf16[256,32,128]{2,1,0:T(8,128)(2,1)}, u32[]{:S(2)}, u32[]{:S(2)}) async-start(bf16[256,32,128]{2,1,0:T(8,128)(2,1)} %copy-done.4), calls=%async_computation.2 | async-start | bytes 4194304 | tf_op jit(solution)/shard_map/all_to_all | solution.py:289
  65.8 14.5 %collective-permute-start.6 = (bf16[64,32,128]{2,1,0:T(8,128)(2,1)}, bf16[64,32,128]{2,1,0:T(8,128)(2,1)}, u32[]{:S(2)}, u32[]{:S(2)}) collective-permute-start(bf16[64,32,128]{2,1,0:T(8,128)(2,1)} %get-tuple-element.52), channel_id=1, source_target_pairs={{0,1},{1,2},{2,3},{3,0},{4,5},{5,6},{6,7},{7,4},{8,9},{9,10},{10,1... | collective-permute-start | bytes 1572872 | tf_op jit(solution)/shard_map/ppermute | solution.py:38
  66.7 25.3 %collective-permute-start.7 = (bf16[64,32,128]{2,1,0:T(8,128)(2,1)}, bf16[64,32,128]{2,1,0:T(8,128)(2,1)}, u32[]{:S(2)}, u32[]{:S(2)}) collective-permute-start(bf16[64,32,128]{2,1,0:T(8,128)(2,1)} %get-tuple-element.53), channel_id=1, source_target_pairs={{0,2},{1,3},{2,0},{3,1},{4,6},{5,7},{6,4},{7,5},{8,10},{9,11},{10,... | collective-permute-start | bytes 1572872 | tf_op jit(solution)/shard_map/ppermute | solution.py:38
  69.1 22.9 %collective-permute-start.8 = (bf16[64,32,128]{2,1,0:T(8,128)(2,1)}, bf16[64,32,128]{2,1,0:T(8,128)(2,1)}, u32[]{:S(2)}, u32[]{:S(2)}) collective-permute-start(bf16[64,32,128]{2,1,0:T(8,128)(2,1)} %get-tuple-element.54), channel_id=1, source_target_pairs={{0,3},{1,0},{2,1},{3,2},{4,7},{5,4},{6,5},{7,6},{8,11},{9,8},{10,9... | collective-permute-start | bytes 1572872 | tf_op jit(solution)/shard_map/ppermute | solution.py:38
  70.3 21.7 %collective-permute-start.9 = (bf16[64,32,128]{2,1,0:T(8,128)(2,1)S(1)}, bf16[64,32,128]{2,1,0:T(8,128)(2,1)}, u32[]{:S(2)}, u32[]{:S(2)}) collective-permute-start(bf16[64,32,128]{2,1,0:T(8,128)(2,1)S(1)} %copy-done.6), channel_id=1, source_target_pairs={{0,4},{4,0},{1,5},{5,1},{2,6},{6,2},{3,7},{7,3},{8,12},{12,8},{9,1... | collective-permute-start | bytes 1572872 | tf_op jit(solution)/shard_map/ppermute | solution.py:38
  92.0 75.5 %collective-permute-start.20 = (bf16[16,512,128]{2,1,0:T(8,128)(2,1)}, bf16[16,512,128]{2,1,0:T(8,128)(2,1)}, u32[]{:S(2)}, u32[]{:S(2)}) collective-permute-start(bf16[16,512,128]{2,1,0:T(8,128)(2,1)} %bitcast.57), channel_id=1, source_target_pairs={{0,3},{4,7},{8,11},{12,15},{16,19},{20,23},{24,27},{28,31},{32,35}... | collective-permute-start | bytes 6291464 | tf_op jit(solution)/shard_map/ppermute | solution.py:356
  98.7 68.9 %collective-permute-start.19 = (bf16[16,512,128]{2,1,0:T(8,128)(2,1)}, bf16[16,512,128]{2,1,0:T(8,128)(2,1)}, u32[]{:S(2)}, u32[]{:S(2)}) collective-permute-start(bf16[16,512,128]{2,1,0:T(8,128)(2,1)} %bitcast.58), channel_id=1, source_target_pairs={{0,1},{4,5},{8,9},{12,13},{16,17},{20,21},{24,25},{28,29},{32,33},... | collective-permute-start | bytes 6291464 | tf_op jit(solution)/shard_map/ppermute | solution.py:355
  104.0 20.6 %all-to-all-start.3 = ((bf16[64,32,128]{2,1,0:T(8,128)(2,1)}), bf16[64,32,128]{2,1,0:T(8,128)(2,1)S(1)}, u32[]{:S(2)}, u32[]{:S(2)}) async-start(bf16[64,32,128]{2,1,0:T(8,128)(2,1)} %shard_map.85), calls=%async_computation.3 | async-start | bytes 1048576 | tf_op jit(solution)/shard_map/all_to_all | solution.py:289
  111.1 3.2 %collective-permute-start.10 = (bf16[64,32,128]{2,1,0:T(8,128)(2,1)}, bf16[64,32,128]{2,1,0:T(8,128)(2,1)}, u32[]{:S(2)}, u32[]{:S(2)}) collective-permute-start(bf16[64,32,128]{2,1,0:T(8,128)(2,1)} %collective-permute-done.6.rest_1_), channel_id=1, source_target_pairs={{0,4},{4,0},{1,5},{5,1},{2,6},{6,2},{3,7},{7,3},{8,12},{12,8},{9,1... | collective-permute-start | bytes 1572872 | tf_op jit(solution)/shard_map/ppermute | solution.py:38
  112.4 2.6 collective-permute-start.11
  112.4 3.4 %collective-permute-start.12 = (bf16[64,32,128]{2,1,0:T(8,128)(2,1)}, bf16[64,32,128]{2,1,0:T(8,128)(2,1)}, u32[]{:S(2)}, u32[]{:S(2)}) collective-permute-start(bf16[64,32,128]{2,1,0:T(8,128)(2,1)} %collective-permute-done.8.rest_3_), channel_id=1, source_target_pairs={{0,4},{4,0},{1,5},{5,1},{2,6},{6,2},{3,7},{7,3},{8,12},{12,8},{9,1... | collective-permute-start | bytes 1572872 | tf_op jit(solution)/shard_map/ppermute | solution.py:38
  124.8 7.0 %collective-permute-start.14 = (bf16[8,32,128]{2,1,0:T(8,128)(2,1)S(1)}, bf16[8,32,128]{2,1,0:T(8,128)(2,1)S(1)}, u32[]{:S(2)}, u32[]{:S(2)}) collective-permute-start(bf16[8,32,128]{2,1,0:T(8,128)(2,1)S(1)} %get-tuple-element.64.own), channel_id=1, source_target_pairs={{0,4},{4,8},{8,12},{12,16},{16,20},{20,24},{24,28},{28,32},{32,36}... | collective-permute-start | bytes 196616 | tf_op jit(solution)/shard_map/ppermute | solution.py:348
  129.0 17.3 %collective-permute-start.16 = (bf16[64,32,128]{2,1,0:T(8,128)(2,1)}, bf16[64,32,128]{2,1,0:T(8,128)(2,1)S(1)}, u32[]{:S(2)}, u32[]{:S(2)}) collective-permute-start(bf16[64,32,128]{2,1,0:T(8,128)(2,1)} %get-tuple-element.79), channel_id=1, source_target_pairs={{0,24},{8,0},{16,8},{24,16},{1,25},{9,1},{17,9},{25,17},{2,26},{10... | collective-permute-start | bytes 1572872 | tf_op jit(solution)/shard_map/ppermute | solution.py:38
  129.4 25.4 %collective-permute-start.15 = (bf16[64,32,128]{2,1,0:T(8,128)(2,1)}, bf16[64,32,128]{2,1,0:T(8,128)(2,1)S(1)}, u32[]{:S(2)}, u32[]{:S(2)}) collective-permute-start(bf16[64,32,128]{2,1,0:T(8,128)(2,1)} %get-tuple-element.81), channel_id=1, source_target_pairs={{0,8},{8,16},{16,24},{24,0},{1,9},{9,17},{17,25},{25,1},{2,10},{10... | collective-permute-start | bytes 1572872 | tf_op jit(solution)/shard_map/ppermute | solution.py:38
  131.8 9.0 %collective-permute-start.13 = (bf16[8,32,128]{2,1,0:T(8,128)(2,1)S(1)}, bf16[8,32,128]{2,1,0:T(8,128)(2,1)S(1)}, u32[]{:S(2)}, u32[]{:S(2)}) collective-permute-start(bf16[8,32,128]{2,1,0:T(8,128)(2,1)S(1)} %get-tuple-element.64.own), channel_id=1, source_target_pairs={{4,0},{8,4},{12,8},{16,12},{20,16},{24,20},{28,24},{32,28},{36,32}... | collective-permute-start | bytes 196616 | tf_op jit(solution)/shard_map/ppermute | solution.py:347
  140.8 26.8 %collective-permute-start.21 = (bf16[64,32,128]{2,1,0:T(8,128)(2,1)}, bf16[64,32,128]{2,1,0:T(8,128)(2,1)S(1)}, u32[]{:S(2)}, u32[]{:S(2)}) collective-permute-start(bf16[64,32,128]{2,1,0:T(8,128)(2,1)} %get-tuple-element.80), channel_id=1, source_target_pairs={{0,16},{8,24},{16,0},{24,8},{1,17},{9,25},{17,1},{25,9},{2,18},{10... | collective-permute-start | bytes 1572872 | tf_op jit(solution)/shard_map/ppermute | solution.py:38
  154.8 4.3 %collective-permute-start.18 = (bf16[8,32,128]{2,1,0:T(8,128)(2,1)S(1)}, bf16[8,32,128]{2,1,0:T(8,128)(2,1)S(1)}, u32[]{:S(2)}, u32[]{:S(2)}) collective-permute-start(bf16[8,32,128]{2,1,0:T(8,128)(2,1)S(1)} %shard_map.88.own), channel_id=1, source_target_pairs={{0,4},{4,8},{8,12},{12,16},{16,20},{20,24},{24,28},{28,32},{32,36}... | collective-permute-start | bytes 196616 | tf_op jit(solution)/shard_map/ppermute | solution.py:348
  156.7 8.9 %collective-permute-start.17 = (bf16[8,32,128]{2,1,0:T(8,128)(2,1)S(1)}, bf16[8,32,128]{2,1,0:T(8,128)(2,1)S(1)}, u32[]{:S(2)}, u32[]{:S(2)}) collective-permute-start(bf16[8,32,128]{2,1,0:T(8,128)(2,1)S(1)} %shard_map.88.own), channel_id=1, source_target_pairs={{4,0},{8,4},{12,8},{16,12},{20,16},{24,20},{28,24},{32,28},{36,32}... | collective-permute-start | bytes 196616 | tf_op jit(solution)/shard_map/ppermute | solution.py:347
  170.3 14.2 %collective-permute-start.28 = (bf16[8,512,128]{2,1,0:T(8,128)(2,1)S(1)}, bf16[8,512,128]{2,1,0:T(8,128)(2,1)S(1)}, u32[]{:S(2)}, u32[]{:S(2)}) collective-permute-start(bf16[8,512,128]{2,1,0:T(8,128)(2,1)S(1)} %slice.48), channel_id=1, source_target_pairs={{3,2},{7,6},{11,10},{15,14},{19,18},{23,22},{27,26},{31,30},{35,34... | collective-permute-start | bytes 3145736 | tf_op jit(solution)/shard_map/ppermute | solution.py:377
  171.1 13.5 %collective-permute-start.27 = (bf16[8,512,128]{2,1,0:T(8,128)(2,1)S(1)}, bf16[8,512,128]{2,1,0:T(8,128)(2,1)S(1)}, u32[]{:S(2)}, u32[]{:S(2)}) collective-permute-start(bf16[8,512,128]{2,1,0:T(8,128)(2,1)S(1)} %slice.47), channel_id=1, source_target_pairs={{1,2},{5,6},{9,10},{13,14},{17,18},{21,22},{25,26},{29,30},{33,34}... | collective-permute-start | bytes 3145736 | tf_op jit(solution)/shard_map/ppermute | solution.py:377
  171.8 4.4 %collective-permute-start.23 = (bf16[8,32,128]{2,1,0:T(8,128)(2,1)S(1)}, bf16[8,32,128]{2,1,0:T(8,128)(2,1)S(1)}, u32[]{:S(2)}, u32[]{:S(2)}) collective-permute-start(bf16[8,32,128]{2,1,0:T(8,128)(2,1)S(1)} %shard_map.89.own), channel_id=1, source_target_pairs={{0,4},{4,8},{8,12},{12,16},{16,20},{20,24},{24,28},{28,32},{32,36}... | collective-permute-start | bytes 196616 | tf_op jit(solution)/shard_map/ppermute | solution.py:348
  173.7 8.9 %collective-permute-start.22 = (bf16[8,32,128]{2,1,0:T(8,128)(2,1)S(1)}, bf16[8,32,128]{2,1,0:T(8,128)(2,1)S(1)}, u32[]{:S(2)}, u32[]{:S(2)}) collective-permute-start(bf16[8,32,128]{2,1,0:T(8,128)(2,1)S(1)} %shard_map.89.own), channel_id=1, source_target_pairs={{4,0},{8,4},{12,8},{16,12},{20,16},{24,20},{28,24},{32,28},{36,32}... | collective-permute-start | bytes 196616 | tf_op jit(solution)/shard_map/ppermute | solution.py:347
  197.9 1.9 collective-permute-start.29
  202.8 20.0 %all-to-all-start.5 = ((bf16[64,32,128]{2,1,0:T(8,128)(2,1)}), bf16[64,32,128]{2,1,0:T(8,128)(2,1)S(1)}, u32[]{:S(2)}, u32[]{:S(2)}) async-start(bf16[64,32,128]{2,1,0:T(8,128)(2,1)} %copy-done.5), calls=%async_computation.5 | async-start | bytes 1048576 | tf_op jit(solution)/shard_map/all_to_all | solution.py:289
  207.3 11.0 %collective-permute-start.26 = (bf16[8,32,128]{2,1,0:T(8,128)(2,1)S(1)}, bf16[8,32,128]{2,1,0:T(8,128)(2,1)S(1)}, u32[]{:S(2)}, u32[]{:S(2)}) collective-permute-start(bf16[8,32,128]{2,1,0:T(8,128)(2,1)S(1)} %shard_map.90.current.refs_0_), channel_id=1, source_target_pairs={{0,3},{1,0},{2,1},{3,2},{4,7},{5,4},{6,5},{7,6},{8,11},{9,8},{10,9... | collective-permute-start | bytes 196616 | tf_op jit(solution)/shard_map/ppermute | solution.py:38
  213.8 6.0 %collective-permute-start.25 = (bf16[8,32,128]{2,1,0:T(8,128)(2,1)S(1)}, bf16[8,32,128]{2,1,0:T(8,128)(2,1)S(1)}, u32[]{:S(2)}, u32[]{:S(2)}) collective-permute-start(bf16[8,32,128]{2,1,0:T(8,128)(2,1)S(1)} %shard_map.90.current.refs_0_), channel_id=1, source_target_pairs={{0,2},{1,3},{2,0},{3,1},{4,6},{5,7},{6,4},{7,5},{8,10},{9,11},{10,... | collective-permute-start | bytes 196616 | tf_op jit(solution)/shard_map/ppermute | solution.py:38
  217.9 4.3 %collective-permute-start.24 = (bf16[8,32,128]{2,1,0:T(8,128)(2,1)S(1)}, bf16[8,32,128]{2,1,0:T(8,128)(2,1)S(1)}, u32[]{:S(2)}, u32[]{:S(2)}) collective-permute-start(bf16[8,32,128]{2,1,0:T(8,128)(2,1)S(1)} %shard_map.90.current.refs_0_), channel_id=1, source_target_pairs={{0,1},{1,2},{2,3},{3,0},{4,5},{5,6},{6,7},{7,4},{8,9},{9,10},{10,1... | collective-permute-start | bytes 196616 | tf_op jit(solution)/shard_map/ppermute | solution.py:38
  223.0 10.3 %collective-permute-start.31 = (bf16[8,32,128]{2,1,0:T(8,128)(2,1)S(1)}, bf16[8,32,128]{2,1,0:T(8,128)(2,1)S(1)}, u32[]{:S(2)}, u32[]{:S(2)}) collective-permute-start(bf16[8,32,128]{2,1,0:T(8,128)(2,1)S(1)} %get-tuple-element.77.own), channel_id=1, source_target_pairs={{0,4},{4,8},{8,12},{12,16},{16,20},{20,24},{24,28},{28,32},{32,36}... | collective-permute-start | bytes 196616 | tf_op jit(solution)/shard_map/ppermute | solution.py:348
  231.4 8.9 %collective-permute-start.30 = (bf16[8,32,128]{2,1,0:T(8,128)(2,1)S(1)}, bf16[8,32,128]{2,1,0:T(8,128)(2,1)S(1)}, u32[]{:S(2)}, u32[]{:S(2)}) collective-permute-start(bf16[8,32,128]{2,1,0:T(8,128)(2,1)S(1)} %get-tuple-element.77.own), channel_id=1, source_target_pairs={{4,0},{8,4},{12,8},{16,12},{20,16},{24,20},{28,24},{32,28},{36,32}... | collective-permute-start | bytes 196616 | tf_op jit(solution)/shard_map/ppermute | solution.py:347
  242.2 35.8 %copy-start.9 = (bf16[8,32,128]{2,1,0:T(8,128)(2,1)S(1)}, bf16[8,32,128]{2,1,0:T(8,128)(2,1)}, u32[]{:S(2)}) copy-start(bf16[8,32,128]{2,1,0:T(8,128)(2,1)} %copy-done.8) | copy-start | bytes 196612
  242.2 35.8 %copy-start.11 = (bf16[8,32,128]{2,1,0:T(8,128)(2,1)S(1)}, bf16[8,32,128]{2,1,0:T(8,128)(2,1)}, u32[]{:S(2)}) copy-start(bf16[8,32,128]{2,1,0:T(8,128)(2,1)} %copy-done.10) | copy-start | bytes 196612
  242.2 35.8 %copy-start.13 = (bf16[8,32,128]{2,1,0:T(8,128)(2,1)S(1)}, bf16[8,32,128]{2,1,0:T(8,128)(2,1)}, u32[]{:S(2)}) copy-start(bf16[8,32,128]{2,1,0:T(8,128)(2,1)} %copy-done.12) | copy-start | bytes 196612
  242.2 4.5 %collective-permute-start.33 = (bf16[8,32,128]{2,1,0:T(8,128)(2,1)S(1)}, bf16[8,32,128]{2,1,0:T(8,128)(2,1)S(1)}, u32[]{:S(2)}, u32[]{:S(2)}) collective-permute-start(bf16[8,32,128]{2,1,0:T(8,128)(2,1)S(1)} %shard_map.94.own), channel_id=1, source_target_pairs={{0,4},{4,8},{8,12},{12,16},{16,20},{20,24},{24,28},{28,32},{32,36}... | collective-permute-start | bytes 196616 | tf_op jit(solution)/shard_map/ppermute | solution.py:348
  244.3 8.9 %collective-permute-start.32 = (bf16[8,32,128]{2,1,0:T(8,128)(2,1)S(1)}, bf16[8,32,128]{2,1,0:T(8,128)(2,1)S(1)}, u32[]{:S(2)}, u32[]{:S(2)}) collective-permute-start(bf16[8,32,128]{2,1,0:T(8,128)(2,1)S(1)} %shard_map.94.own), channel_id=1, source_target_pairs={{4,0},{8,4},{12,8},{16,12},{20,16},{24,20},{28,24},{32,28},{36,32}... | collective-permute-start | bytes 196616 | tf_op jit(solution)/shard_map/ppermute | solution.py:347
  255.1 4.6 %collective-permute-start.35 = (bf16[8,32,128]{2,1,0:T(8,128)(2,1)S(1)}, bf16[8,32,128]{2,1,0:T(8,128)(2,1)S(1)}, u32[]{:S(2)}, u32[]{:S(2)}) collective-permute-start(bf16[8,32,128]{2,1,0:T(8,128)(2,1)S(1)} %shard_map.95.own), channel_id=1, source_target_pairs={{0,4},{4,8},{8,12},{12,16},{16,20},{20,24},{24,28},{28,32},{32,36}... | collective-permute-start | bytes 196616 | tf_op jit(solution)/shard_map/ppermute | solution.py:348
  257.0 8.9 %collective-permute-start.34 = (bf16[8,32,128]{2,1,0:T(8,128)(2,1)S(1)}, bf16[8,32,128]{2,1,0:T(8,128)(2,1)S(1)}, u32[]{:S(2)}, u32[]{:S(2)}) collective-permute-start(bf16[8,32,128]{2,1,0:T(8,128)(2,1)S(1)} %shard_map.95.own), channel_id=1, source_target_pairs={{4,0},{8,4},{12,8},{16,12},{20,16},{24,20},{28,24},{32,28},{36,32}... | collective-permute-start | bytes 196616 | tf_op jit(solution)/shard_map/ppermute | solution.py:347
  267.9 6.2 %collective-permute-start.38 = (bf16[8,32,128]{2,1,0:T(8,128)(2,1)S(1)}, bf16[8,32,128]{2,1,0:T(8,128)(2,1)S(1)}, u32[]{:S(2)}, u32[]{:S(2)}) collective-permute-start(bf16[8,32,128]{2,1,0:T(8,128)(2,1)S(1)} %shard_map.96.refs_4_), channel_id=1, source_target_pairs={{0,3},{1,0},{2,1},{3,2},{4,7},{5,4},{6,5},{7,6},{8,11},{9,8},{10,9... | collective-permute-start | bytes 196616 | tf_op jit(solution)/shard_map/ppermute | solution.py:38
  269.6 5.7 %collective-permute-start.37 = (bf16[8,32,128]{2,1,0:T(8,128)(2,1)S(1)}, bf16[8,32,128]{2,1,0:T(8,128)(2,1)S(1)}, u32[]{:S(2)}, u32[]{:S(2)}) collective-permute-start(bf16[8,32,128]{2,1,0:T(8,128)(2,1)S(1)} %shard_map.96.refs_4_), channel_id=1, source_target_pairs={{0,2},{1,3},{2,0},{3,1},{4,6},{5,7},{6,4},{7,5},{8,10},{9,11},{10,... | collective-permute-start | bytes 196616 | tf_op jit(solution)/shard_map/ppermute | solution.py:38
  273.6 4.3 %collective-permute-start.36 = (bf16[8,32,128]{2,1,0:T(8,128)(2,1)S(1)}, bf16[8,32,128]{2,1,0:T(8,128)(2,1)S(1)}, u32[]{:S(2)}, u32[]{:S(2)}) collective-permute-start(bf16[8,32,128]{2,1,0:T(8,128)(2,1)S(1)} %shard_map.96.refs_4_), channel_id=1, source_target_pairs={{0,1},{1,2},{2,3},{3,0},{4,5},{5,6},{6,7},{7,4},{8,9},{9,10},{10,1... | collective-permute-start | bytes 196616 | tf_op jit(solution)/shard_map/ppermute | solution.py:38
  (14 other events, 80.1 us)
where the time goes:
time: 281 us; the launch traced here: 279 us
  starting transfers between devices  112 us (40%)
  waiting for transfers between devices  80.5 us (29%)
  Pallas kernels  41.9 us (15%)
  local copies, waits for them, and re-layouts  29.8 us (11%)
  blocking collectives  12 us (4%)
    ppermute x6, waiting for transfers between devices, one_sweep(): right = lax.ppermute(current, BLK, [(i + 1, i) for i in range(ends)])  39.7 us
    ppermute x22, starting transfers between devices, shift(): lax.ppermute(value, axis, [(i, (i + distance) % count) for i in range(cou...  39.5 us
    ppermute x22, waiting for transfers between devices, shift(): lax.ppermute(value, axis, [(i, (i + distance) % count) for i in range(cou...  38.9 us
    all_to_all x5, starting transfers between devices, exchange(): return lax.all_to_all(value, axis, split_axis=0, concat_axis=0, tiled=True)  24.2 us
    ppermute x6, starting transfers between devices, one_sweep(): left = lax.ppermute(current, BLK, [(i, i + 1) for i in range(ends)])  20.4 us
    pallas_call x2, Pallas kernels, parcels(): pl.pallas_call(parcels_kernel, grid=(4,), in_specs=[SM, SM, pl.BlockSpec(...  14 us
    ppermute x6, starting transfers between devices, one_sweep(): right = lax.ppermute(current, BLK, [(i + 1, i) for i in range(ends)])  13.7 us
    all_to_all x1, blocking collectives, exchange(): return lax.all_to_all(value, axis, split_axis=0, concat_axis=0, tiled=True)  12 us
  transfers between devices with their start and end apart: 44, of which 21 were waited for; matrix products, arithmetic and copies ran while one was open for 8% of the time, Pallas kernels for 10%

commit v1 on v0

--- a/solution.py
+++ b/solution.py
@@ -17,7 +17,6 @@
 VM = pl.BlockSpec(memory_space=pltpu.VMEM)
 SM = pl.BlockSpec(memory_space=pltpu.SMEM)
 ANY = pl.BlockSpec(memory_space=pl.ANY)
-HBM = pl.BlockSpec(memory_space=pltpu.HBM)
 BLK = ("z", "y", "c")
 
 
@@ -44,7 +43,7 @@
     for j in range(16):
         total = None
         for i in range(4):
-            source = src_ref[k, 0, j, i]
+            source = src_ref[k, 0, i, j]
             term = jnp.dot(inter_ref[0, j, i], past_ref[0, source], preferred_element_type=F32)
             total = term if total is None else total + term
         turned = total.T.astype(BF)
@@ -80,30 +79,40 @@
     )(first, sources, past, coupling)
 
 
-def place_kernel(per, places_ref, *rest):
-    ins, (out_ref, dense, sem) = rest[:-3], rest[-3:]
+def place_kernel(count, places_ref, *rest):
+    ins, (out_ref, held, dense, sems) = rest[:count], rest[count:]
+    per = held.shape[1]
+    arriving = [pltpu.make_async_copy(ins[n], held.at[n], sems.at[n]) for n in range(count)]
+    for copy in arriving:
+        copy.start()
     dense[...] = jnp.zeros_like(dense)
-    for n, values in enumerate(ins):
-
-        def body(p, carry, n=n, values=values):
+    for n in range(count):
+        arriving[n].wait()
+
+        def body(p, carry, n=n):
             at = places_ref[n * per + p]
-            dense[at] = dense[at] + values[p]
+            dense[at] = dense[at] + held[n, p]
             return carry
 
         lax.fori_loop(0, per, body, 0, unroll=8)
-    copy = pltpu.make_async_copy(dense.at[pl.ds(0, 256)], out_ref, sem)
-    copy.start()
-    copy.wait()
+    leaving = pltpu.make_async_copy(dense.at[pl.ds(0, 256)], out_ref, sems.at[count])
+    leaving.start()
+    leaving.wait()
 
 
 def place(places, buffers):
-    return pl.pallas_call(
-        functools.partial(place_kernel, buffers[0].shape[0]),
-        in_specs=[SM] + [VM] * len(buffers),
-        out_specs=HBM,
+    count, per = len(buffers), buffers[0].shape[0]
+    return pl.pallas_call(
+        functools.partial(place_kernel, count),
+        in_specs=[SM] + [ANY] * count,
+        out_specs=ANY,
         out_shape=shape(256, RW, B),
-        scratch_shapes=[pltpu.VMEM((257, RW, B), BF), pltpu.SemaphoreType.DMA],
-        compiler_params=params(),
+        scratch_shapes=[
+            pltpu.VMEM((count, per, RW, B), BF),
+            pltpu.VMEM((257, RW, B), BF),
+            pltpu.SemaphoreType.DMA((count + 1,)),
+        ],
+        compiler_params=params(60),
         cost_estimate=cost(1, 1),
     )(places, *buffers)
 
@@ -127,26 +136,18 @@
     )(halves)
 
 
-def add_late_kernel(y_ref, places_ref, dense_ref, *rest):
-    others, late, (out_ref, total, own, sem) = rest[:3], rest[3:5], rest[5:]
-    start = pl.multiple_of(y_ref[0] * 64, 64)
-    copy = pltpu.make_async_copy(dense_ref.at[pl.ds(start, 64)], own, sem)
-    copy.start()
+def add_late_kernel(places_ref, halves, first, second, out_ref, total):
     for n in range(NZ):
         part = pl.ds(n * BLKS, BLKS)
-        total[part] = sum(value[part].astype(F32) for value in others)
-    copy.wait()
-    for n in range(NZ):
-        part = pl.ds(n * BLKS, BLKS)
-        total[part] = total[part] + own[part].astype(F32)
-    for n in range(2):
-
-        def body(p, carry, n=n):
+        total[part] = sum(halves[pl.ds(m * 64 + n * BLKS, BLKS)].astype(F32) for m in range(NY))
+    for n, late in enumerate((first, second)):
+
+        def body(p, carry, n=n, late=late):
             at = places_ref[n * 64 + p]
 
             @pl.when(at < 64)
             def _():
-                total[at] = total[at] + late[n][p].astype(F32)
+                total[at] = total[at] + late[p].astype(F32)
 
             return carry
 
@@ -156,20 +157,16 @@
         out_ref[part] = total[part].astype(BF)
 
 
-def add_late(y, places, dense, others, late):
+def add_late(places, halves, first, second):
     return pl.pallas_call(
         add_late_kernel,
-        in_specs=[SM, SM, ANY] + [VM] * 5,
+        in_specs=[SM] + [VM] * 3,
         out_specs=VM,
         out_shape=shape(64, RW, B),
-        scratch_shapes=[
-            pltpu.VMEM((64, RW, B), F32),
-            pltpu.VMEM((64, RW, B), BF),
-            pltpu.SemaphoreType.DMA,
-        ],
-        compiler_params=params(),
-        cost_estimate=cost(1, 1),
-    )(y, places, dense, *others, *late)
+        scratch_shapes=[pltpu.VMEM((64, RW, B), F32)],
+        compiler_params=params(),
+        cost_estimate=cost(1, 1),
+    )(places, halves, first, second)
 
 
 def total_of(ref, count):
@@ -198,7 +195,7 @@
     )(pieces, incident, inverse)
 
 
-def sweep_kernel(ids_ref, right, own, left, drive_ref, near_ref, inverse, out_ref, held):
+def sweep_kernel(ids_ref, left, own, right, drive_ref, near_ref, inverse, out_ref, held):
     held[0:BLKS] = left[...]
     held[BLKS : 2 * BLKS] = own[...]
     held[2 * BLKS : 3 * BLKS] = right[...]
@@ -209,7 +206,7 @@
         out_ref[g] = jnp.dot(rest, inverse[g], preferred_element_type=F32).astype(BF)
 
 
-def sweep(ids, right, own, left, drive, near, inverse):
+def sweep(ids, left, own, right, drive, near, inverse):
     return pl.pallas_call(
         sweep_kernel,
         in_specs=[SM] + [VM] * 6,
@@ -218,49 +215,41 @@
         scratch_shapes=[pltpu.VMEM((3 * BLKS, RW, B), BF)],
         compiler_params=params(),
         cost_estimate=cost(1, 1),
-    )(ids, right, own, left, drive, near, inverse)
-
-
-def late_parcels_kernel(x_ref, src_ref, current, *rest):
-    (own, low, high, *far), (out_ref, coupling, sem) = rest[:5], rest[5:]
-    x = x_ref[0]
-    for half in range(2):
-        part = pl.ds(half * 8, 8)
-        choices = (own.at[part], low.at[part], far[half], high.at[part])
-        for who, source in enumerate(choices):
-
-            @pl.when(x == who)
-            def _(part=part, half=half, source=source):
-                pltpu.make_async_copy(source, coupling.at[part], sem.at[half]).start()
-
-    for half in range(2):
-        part = coupling.at[pl.ds(half * 8, 8)]
-        pltpu.make_async_copy(part, part, sem.at[half]).wait()
-        for j in range(half * 8, half * 8 + 8):
-            gathered = jnp.concatenate([current[src_ref[j * 4 + i]] for i in range(4)], axis=1)
-            parcel = jnp.dot(gathered, coupling[j], preferred_element_type=F32).astype(BF)
-            for copy in range(NY):
-                out_ref[copy * 16 + j] = parcel
-
-
-def late_parcels(x, sources, current, couplings):
+    )(ids, left, own, right, drive, near, inverse)
+
+
+def gather_waves(x, pieces, whole):
+    for distance, piece in enumerate(pieces):
+        start = pl.multiple_of(lax.rem(x + NX - distance, NX) * RW, RW)
+        whole[:, pl.ds(start, RW), :] = piece[...]
+
+
+def late_parcels_kernel(x_ref, src_ref, *rest):
+    pieces, coupling, outs, whole = rest[:4], rest[4], rest[5:9], rest[9]
+    gather_waves(x_ref[0], pieces, whole)
+    for j in range(16):
+        gathered = jnp.concatenate([whole[src_ref[i * 16 + j]] for i in range(4)], axis=1)
+        parcel = jnp.dot(gathered, coupling[j], preferred_element_type=F32).astype(BF)
+        for n in range(NX):
+            outs[n][j] = parcel[n * RW : (n + 1) * RW]
+
+
+def late_parcels(x, sources, pieces, coupling):
     return pl.pallas_call(
         late_parcels_kernel,
-        in_specs=[SM, SM, VM] + [ANY] * 5,
-        out_specs=VM,
-        out_shape=shape(NY * 16, RW, B),
-        scratch_shapes=[pltpu.VMEM((16, 4 * B, B), BF), pltpu.SemaphoreType.DMA((2,))],
-        compiler_params=params(),
-        cost_estimate=cost(1, 1),
-    )(x, sources, current, *couplings)
+        in_specs=[SM, SM] + [VM] * 5,
+        out_specs=[VM] * NX,
+        out_shape=[shape(16, RW, B)] * NX,
+        scratch_shapes=[pltpu.VMEM((BLKS, B, B), BF)],
+        compiler_params=params(),
+        cost_estimate=cost(1, 1),
+    )(x, sources, *pieces, coupling)
 
 
 def finish_kernel(x_ref, *refs):
     ins, out_ref, held = refs[:8], refs[8], refs[9]
     for step in range(2):
-        for distance in range(4):
-            start = pl.multiple_of(lax.rem(x_ref[0] + NX - distance, NX) * RW, RW)
-            held[:, pl.ds(start, RW), :] = ins[step * 4 + distance][...]
+        gather_waves(x_ref[0], ins[step * NX : (step + 1) * NX], held)
         for g in range(BLKS):
             out_ref[step, g] = held[g].T
 
@@ -296,15 +285,17 @@
     past = history.reshape(4, BLKS, B, B)
     coupling = inter[:, 0]
 
-    meta = jnp.concatenate([dest_blocks[:, 0].reshape(64), src_lists[0, 0].reshape(64)])
+    meta = jnp.concatenate([dest_blocks[:, 0].reshape(64), src_lists[0, 0].T.reshape(64)])
     metas = exchange(jnp.broadcast_to(meta[None], (NX, 128)), "x")
 
-    older = lax.ppermute(past[3], "x", [(i, i + 1) for i in range(NX - 1)])
-    (sent,) = parcels(x_scalar, src_lists, past, coupling, False)
+    older = shift(past[3], "x", 1)
+    sources = src_lists.swapaxes(2, 3)
+    (sent,) = parcels(x_scalar, sources, past, coupling, False)
     sent = after(sent, older, metas)
     crossed = exchange(sent, "x")
-    later_past = jnp.concatenate([after(older, sent)[None], past[:3]], 0)
-    later_sent = parcels(x_scalar, src_lists, later_past, coupling, True)
+    older = jnp.where(x == 0, jnp.zeros_like(older), after(older, sent))
+    later_past = jnp.concatenate([older[None], past[:3]], 0)
+    later_sent = parcels(x_scalar, sources, later_past, coupling, True)
 
     metas = after(metas, sent)
     metas = jnp.stack([metas, shift(metas, "c", 1)])
@@ -329,7 +320,7 @@
     crossed = crossed.reshape(256, RW, B)
     dense = place(places, [crossed, shift(crossed, "c", 1)])
     halves = exchange(dense, "y")
-    later_sent = after(later_sent, dense)
+    later_sent = after(later_sent, crossed)
     steps = (0, 1, 2, -1)
     later_crossed = [later_sent[0]] + [
         shift(later_sent[n], "x", steps[n]) for n in range(1, NX)
@@ -343,47 +334,35 @@
     ids = (nbr_ids - (position - 1) * BLKS).reshape(64)
 
     def one_sweep(current, drive):
-        ends = NZ * NY * NC - 1
-        right = lax.ppermute(current, BLK, [(i + 1, i) for i in range(ends)])
-        left = lax.ppermute(current, BLK, [(i, i + 1) for i in range(ends)])
-        return sweep(ids, right, current, left, drive, near_t, inverse_t)
+        right = shift(current, BLK, -1)
+        left = shift(current, BLK, 1)
+        return sweep(ids, left, current, right, drive, near_t, inverse_t)
 
     later_own = shift(later_crossed[0], "c", 1)
     later_crossed = after(later_crossed, near_t, inverse_t, incident, ids, later_own)
 
-    start = after(newest, later_crossed)
-    low = lax.ppermute(start, "x", [(0, 1)])
-    high = lax.ppermute(start, "x", [(0, 3)])
-    halves = after(halves, later_crossed, later_own, near_t, inverse_t, incident, ids)
+    halves = after(halves, later_crossed)
     summed = add(halves)
     pieces = exchange(summed, "z")
 
     later_other = [later_own] + [shift(value, "c", 1) for value in later_crossed[1:]]
     later_dense = place(by_distance, later_crossed + later_other)
 
-    def other_part(distance):
-        start = (y + distance) % NY * 64
-        return lax.dynamic_slice_in_dim(later_dense, start, 64, axis=0)
-
-    parts = [other_part(n) for n in range(1, NY)]
-    pieces = after(pieces, later_dense, parts)
-    later_halves = [shift(parts[n], "y", steps[n + 1]) for n in range(3)]
-
+    pieces = after(pieces, later_dense)
     drive, current = first_solve(pieces, incident[0], inverse_t)
-    current = one_sweep(current, drive)
-    current = after(current, later_halves[0], later_halves[2])
-    current = one_sweep(current, drive)
-    current, low, high = after((current, low, high), later_halves[1])
-    far = [lax.ppermute(low[:8], "x", [(1, 2)]), lax.ppermute(high[8:], "x", [(3, 2)])]
-    current = one_sweep(current, drive)
+    for _ in range(SWEEPS):
+        current = one_sweep(current, drive)
+    later_halves = exchange(after(later_dense, current), "y")
     outputs = spread(current, "x")
 
-    couplings = after([newest, low, high] + far, current)
-    late = exchange(late_parcels(x_scalar, late_sources, current, couplings), "y")
-    y_scalar = y.astype(jnp.int32).reshape(1)
-    late = [late, shift(late, "c", 1)]
-    pieces = exchange(add_late(y_scalar, late_places, later_dense, later_halves, late), "z")
-    pieces = after(pieces, outputs)
+    late = late_parcels(x_scalar, late_sources, outputs, newest)
+    late = [late[0], shift(late[1], "x", 1), shift(late[2], "x", 2), shift(late[3], "x", -1)]
+    mine = late[3]
+    for n in range(NX - 2, -1, -1):
+        mine = jnp.where(x == n, late[n], mine)
+    mine = jnp.broadcast_to(mine[None], (NY,) + mine.shape).reshape(NY * 16, RW, B)
+    mine = exchange(after(mine, later_halves), "y")
+    pieces = exchange(add_late(late_places, later_halves, mine, shift(mine, "c", 1)), "z")
     drive, current = first_solve(pieces, incident[1], inverse_t)
     for _ in range(SWEEPS):
         current = one_sweep(current, drive)

time: 281 us -> 250 us (0.89)
  the two profiles are of different devices: /device:TPU:121 before, /device:TPU:4 now
where the time goes in v1:
time: 250 us; the launch traced here: 249 us
  waiting for transfers between devices  88.5 us (35%)
  starting transfers between devices  54.5 us (22%)
  Pallas kernels  47.1 us (19%)
  blocking collectives  34.6 us (14%)
  local copies, waits for them, and re-layouts  20.4 us (8%)
  other arithmetic  3.74 us (1%)
    ppermute x35, waiting for transfers between devices, shift(): lax.ppermute(value, axis, [(i, (i + distance) % count) for i in range(cou...  81.5 us
    all_to_all x2, blocking collectives, exchange(): return lax.all_to_all(value, axis, split_axis=0, concat_axis=0, tiled=True)  34.6 us
    all_to_all x5, starting transfers between devices, exchange(): return lax.all_to_all(value, axis, split_axis=0, concat_axis=0, tiled=True)  27.7 us
    ppermute x35, starting transfers between devices, shift(): lax.ppermute(value, axis, [(i, (i + distance) % count) for i in range(cou...  26.8 us
    pallas_call x2, Pallas kernels, parcels(): pl.pallas_call(parcels_kernel, grid=(4,), in_specs=[SM, SM, pl.BlockSpec(...  14.1 us
    pallas_call x2, Pallas kernels, place(): pl.pallas_call(functools.partial(place_kernel, count), in_specs=[SM] + [A...  12.3 us
    pallas_call x6, Pallas kernels, sweep(): pl.pallas_call(sweep_kernel, in_specs=[SM] + [VM] * 6, out_specs=VM, out_...  11.5 us
    all_to_all x5, waiting for transfers between devices, exchange(): return lax.all_to_all(value, axis, split_axis=0, concat_axis=0, tiled=True)  7 us
  transfers between devices with their start and end apart: 40, of which 32 were waited for; matrix products, arithmetic and copies ran while one was open for 7% of the time, Pallas kernels for 9%

profile of v1, /device:TPU:4, one launch (start us, length us, event | category | flops | bytes accessed | tf_op | source)
XLA Modules:
  0.0 249.1 jit_solution(6736110062147529450)
XLA Ops:
  3.4 5.4 %all-to-all-start = ((s32[4,1,128]{2,1,0:T(1,128)}), s32[4,1,128]{2,1,0:T(1,128)S(1)}, u32[]{:S(2)}, u32[]{:S(2)}) async-start(s32[4,1,128]{2,1,0:T(1,128)} %broadcast_in_dim.37), calls=%async_computation | async-start | bytes 4096 | tf_op jit(solution)/shard_map/all_to_all | solution.py:278
  11.1 7.1 %shard_map.82 = bf16[4,64,32,128]{3,2,1,0:T(8,128)(2,1)} custom-call(s32[1]{0:T(128)} %bitcast.first_ref.x_ref, s32[4,1,4,16]{3,2,1,0:T(4,128)} %bitcast.73, bf16[4,8,128,128]{3,2,1,0:T(8,128)(2,1)} %bitcast.67, bf16[4,16,4,128,128]{4,3,2,1,0:T(8,128)(2,1)} %bitcast.62), custom_call_target="tpu_custom_call" | custom-call | flops 1 | bytes 1 | tf_op jit(solution)/shard_map/pallas_call | solution.py:65
  19.0 4.8 %all-to-all-start.1 = ((bf16[4,64,32,128]{3,2,1,0:T(8,128)(2,1)}), bf16[4,64,32,128]{3,2,1,0:T(8,128)(2,1)S(1)}, u32[]{:S(2)}, u32[]{:S(2)}) async-start(bf16[4,64,32,128]{3,2,1,0:T(8,128)(2,1)} %shard_map.82), calls=%async_computation.1 | async-start | bytes 4194304 | tf_op jit(solution)/shard_map/all_to_all | solution.py:278
  23.8 3.2 %slice_bitcast_fusion = bf16[16,4,128,128]{3,2,1,0:T(8,128)(2,1)} fusion(bf16[4,1,16,4,128,128]{5,4,3,2,1,0:T(8,128)(2,1)} %param.10), kind=kLoop, calls=%fused_computation.2 | loop fusion | bytes 4194304 | tf_op jit(solution)/shard_map/squeeze | solution.py:318
  28.2 7.0 %shard_map.83 = (bf16[64,32,128]{2,1,0:T(8,128)(2,1)}, bf16[64,32,128]{2,1,0:T(8,128)(2,1)}, bf16[64,32,128]{2,1,0:T(8,128)(2,1)}, bf16[64,32,128]{2,1,0:T(8,128)(2,1)}) custom-call(s32[1]{0:T(128)} %bitcast.first_ref.x_ref, s32[4,1,4,16]{3,2,1,0:T(4,128)} %bitcast.74, bf16[4,8,128,128]{3,2,1,0:T(8,128)(2,1)} %pad_maximum_fusion.past_ref, ...), custom_call_target="tpu_custom_call" | custom-call | flops 1 | bytes 1 | tf_op jit(solution)/shard_map/pallas_call | solution.py:65
  35.2 3.9 %copy.26 = bf16[16,4,128,128]{3,2,1,0:T(8,128)(2,1)} copy(bf16[16,4,128,128]{2,3,1,0:T(8,128)(2,1)} %bitcast.66) | data formatting | bytes 4194304 | tf_op jit(solution)/shard_map/transpose | solution.py:318
  39.1 2.5 collective-permute-start.4
  45.1 1.5 collective-permute-done.3
  47.9 4.3 %collective-permute-done.5.rest_1_ = bf16[256,32,128]{2,1,0:T(8,128)(2,1)} collective-permute-done((bf16[256,32,128]{2,1,0:T(8,128)(2,1)S(1)}, bf16[256,32,128]{2,1,0:T(8,128)(2,1)}, u32[]{:S(2)}, u32[]{:S(2)}) %collective-permute-start.5) | collective-permute-done | bytes 2097184 | tf_op jit(solution)/shard_map/ppermute | solution.py:37
  52.1 6.4 %shard_map.84 = bf16[256,32,128]{2,1,0:T(8,128)(2,1)} custom-call(s32[512]{0:T(512)} %reshape.160.places_ref, bf16[256,32,128]{2,1,0:T(8,128)(2,1)} %bitcast.65, bf16[256,32,128]{2,1,0:T(8,128)(2,1)} %collective-permute-done.5.rest_1_), custom_call_target="tpu_custom_call" | custom-call | flops 1 | bytes 1 | tf_op jit(solution)/shard_map/pallas_call | solution.py:105
  58.6 4.6 %all-to-all-start.2 = ((bf16[256,32,128]{2,1,0:T(8,128)(2,1)}), bf16[256,32,128]{2,1,0:T(8,128)(2,1)}, u32[]{:S(2)}, u32[]{:S(2)}) async-start(bf16[256,32,128]{2,1,0:T(8,128)(2,1)} %shard_map.84), calls=%async_computation.2 | async-start | bytes 4194304 | tf_op jit(solution)/shard_map/all_to_all | solution.py:278
  68.0 3.0 %copy.27 = bf16[8,8,128,128]{3,2,1,0:T(8,128)(2,1)S(1)} copy(bf16[8,8,128,128]{2,3,1,0:T(8,128)(2,1)} %bitcast.70) | data formatting | bytes 4194304 | tf_op jit(solution)/shard_map/transpose | solution.py:330
  71.1 7.3 %collective-permute-done.6.rest_1_ = bf16[64,32,128]{2,1,0:T(8,128)(2,1)} collective-permute-done((bf16[64,32,128]{2,1,0:T(8,128)(2,1)}, bf16[64,32,128]{2,1,0:T(8,128)(2,1)}, u32[]{:S(2)}, u32[]{:S(2)}) %collective-permute-start.6) | collective-permute-done | bytes 524320 | tf_op jit(solution)/shard_map/ppermute | solution.py:37
  78.3 10.5 %collective-permute-done.7.rest_2_ = bf16[64,32,128]{2,1,0:T(8,128)(2,1)} collective-permute-done((bf16[64,32,128]{2,1,0:T(8,128)(2,1)}, bf16[64,32,128]{2,1,0:T(8,128)(2,1)}, u32[]{:S(2)}, u32[]{:S(2)}) %collective-permute-start.7) | collective-permute-done | bytes 524320 | tf_op jit(solution)/shard_map/ppermute | solution.py:37
  88.8 1.8 collective-permute-done.8.rest_3_
  90.7 2.6 %shard_map.85 = bf16[64,32,128]{2,1,0:T(8,128)(2,1)} custom-call(bf16[256,32,128]{2,1,0:T(8,128)(2,1)} %all-to-all-done.2.halves), custom_call_target="tpu_custom_call" | custom-call | flops 1 | bytes 1 | tf_op jit(solution)/shard_map/pallas_call | solution.py:129
  93.3 8.4 %all-to-all-start.3 = ((bf16[64,32,128]{2,1,0:T(8,128)(2,1)}), bf16[64,32,128]{2,1,0:T(8,128)(2,1)S(1)}, u32[]{:S(2)}, u32[]{:S(2)}) async-start(bf16[64,32,128]{2,1,0:T(8,128)(2,1)} %shard_map.85), calls=%async_computation.3 | async-start | bytes 1048576 | tf_op jit(solution)/shard_map/all_to_all | solution.py:278
  105.5 5.9 %shard_map.86 = bf16[256,32,128]{2,1,0:T(8,128)(2,1)} custom-call(s32[512]{0:T(512)} %reshape.161.places_ref, bf16[64,32,128]{2,1,0:T(8,128)(2,1)} %get-tuple-element.53.rest_0_, bf16[64,32,128]{2,1,0:T(8,128)(2,1)} %collective-permute-done.6.rest_1_, bf16[64,32,128]{2,1,0:T(8,128)(2,1)} %collective-permute-done.7.rest_2_, ...), custom_call_target="tpu_custom_call" | custom-call | flops 1 | bytes 1 | tf_op jit(solution)/shard_map/pallas_call | solution.py:105
  111.4 7.0 %all-to-all-done.3.pieces = bf16[64,32,128]{2,1,0:T(8,128)(2,1)S(1)} async-done(((bf16[64,32,128]{2,1,0:T(8,128)(2,1)}), bf16[64,32,128]{2,1,0:T(8,128)(2,1)S(1)}, u32[]{:S(2)}, u32[]{:S(2)}) %all-to-all-start.3) | async-done | bytes 524320 | tf_op jit(solution)/shard_map/all_to_all | solution.py:278
  120.6 5.2 %collective-permute-done.13.left = bf16[8,32,128]{2,1,0:T(8,128)(2,1)S(1)} collective-permute-done((bf16[8,32,128]{2,1,0:T(8,128)(2,1)S(1)}, bf16[8,32,128]{2,1,0:T(8,128)(2,1)S(1)}, u32[]{:S(2)}, u32[]{:S(2)}) %collective-permute-start.13) | collective-permute-done | bytes 65568 | tf_op jit(solution)/shard_map/ppermute | solution.py:37
  125.8 1.9 shard_map.88.own
  129.6 5.2 %collective-permute-done.15.left = bf16[8,32,128]{2,1,0:T(8,128)(2,1)S(1)} collective-permute-done((bf16[8,32,128]{2,1,0:T(8,128)(2,1)S(1)}, bf16[8,32,128]{2,1,0:T(8,128)(2,1)S(1)}, u32[]{:S(2)}, u32[]{:S(2)}) %collective-permute-start.15) | collective-permute-done | bytes 65568 | tf_op jit(solution)/shard_map/ppermute | solution.py:37
  134.8 1.9 shard_map.89.own
  138.6 5.2 %collective-permute-done.17.left = bf16[8,32,128]{2,1,0:T(8,128)(2,1)S(1)} collective-permute-done((bf16[8,32,128]{2,1,0:T(8,128)(2,1)S(1)}, bf16[8,32,128]{2,1,0:T(8,128)(2,1)S(1)}, u32[]{:S(2)}, u32[]{:S(2)}) %collective-permute-start.17) | collective-permute-done | bytes 65568 | tf_op jit(solution)/shard_map/ppermute | solution.py:37
  143.8 1.9 shard_map.90.rest_0_.refs_0_
  145.7 4.5 %all-to-all-start.4 = ((bf16[256,32,128]{2,1,0:T(8,128)(2,1)}), bf16[256,32,128]{2,1,0:T(8,128)(2,1)}, u32[]{:S(2)}, u32[]{:S(2)}) async-start(bf16[256,32,128]{2,1,0:T(8,128)(2,1)} %shard_map.86), calls=%async_computation.4 | async-start | bytes 4194304 | tf_op jit(solution)/shard_map/all_to_all | solution.py:278
  150.2 1.6 collective-permute-start.21
  151.8 2.9 %collective-permute-start.20 = (bf16[8,32,128]{2,1,0:T(8,128)(2,1)S(1)}, bf16[8,32,128]{2,1,0:T(8,128)(2,1)S(1)}, u32[]{:S(2)}, u32[]{:S(2)}) collective-permute-start(bf16[8,32,128]{2,1,0:T(8,128)(2,1)S(1)} %shard_map.90.rest_0_.refs_0_), channel_id=1, source_target_pairs={{0,2},{1,3},{2,0},{3,1},{4,6},{5,7},{6,4},{7,5},{8,10},{9,11},{10,... | collective-permute-start | bytes 196616 | tf_op jit(solution)/shard_map/ppermute | solution.py:37
  154.8 2.7 %collective-permute-done.20.rest_2_.refs_2_ = bf16[8,32,128]{2,1,0:T(8,128)(2,1)S(1)} collective-permute-done((bf16[8,32,128]{2,1,0:T(8,128)(2,1)S(1)}, bf16[8,32,128]{2,1,0:T(8,128)(2,1)S(1)}, u32[]{:S(2)}, u32[]{:S(2)}) %collective-permute-start.20) | collective-permute-done | bytes 65568 | tf_op jit(solution)/shard_map/ppermute | solution.py:37
  158.9 1.6 copy-done.1
  160.5 2.0 shard_map.91
  163.2 1.5 collective-permute-start.23
  164.7 2.6 %collective-permute-start.24 = (bf16[16,32,128]{2,1,0:T(8,128)(2,1)S(1)}, bf16[16,32,128]{2,1,0:T(8,128)(2,1)}, u32[]{:S(2)}, u32[]{:S(2)}) collective-permute-start(bf16[16,32,128]{2,1,0:T(8,128)(2,1)S(1)} %get-tuple-element.65), channel_id=1, source_target_pairs={{0,3},{1,0},{2,1},{3,2},{4,7},{5,4},{6,5},{7,6},{8,11},{9,8},{10,9... | collective-permute-start | bytes 393224 | tf_op jit(solution)/shard_map/ppermute | solution.py:37
  167.8 2.2 collective-permute-done.23
  172.3 12.6 %all_to_all.39.first = bf16[64,32,128]{2,1,0:T(8,128)(2,1)S(1)} all-to-all(bf16[64,32,128]{2,1,0:T(8,128)(2,1)S(1)} %bitcast.69), channel_id=1, replica_groups=mesh['z'=8,'y'=4,'c'=2,'x'=4] {'y'}, dimensions={0} | all-to-all | bytes 1048576 | tf_op jit(solution)/shard_map/all_to_all | solution.py:278
  184.8 1.9 collective-permute-done.25.second
  186.7 3.2 %shard_map.92 = bf16[64,32,128]{2,1,0:T(8,128)(2,1)S(1)} custom-call(s32[128]{0:T(128)S(1)} %and_select_fusion.8.places_ref, bf16[256,32,128]{2,1,0:T(8,128)(2,1)} %all-to-all-done.4.halves, bf16[64,32,128]{2,1,0:T(8,128)(2,1)S(1)} %all_to_all.39.first, bf16[64,32,128]{2,1,0:T(8,128)(2,1)S(1)} %collective-permute-done.25.second), custom_call_target="tpu_custom_call" | custom-call | flops 1 | bytes 1 | tf_op jit(solution)/shard_map/pallas_call | solution.py:161
  189.9 22.0 %all_to_all.40.pieces = bf16[64,32,128]{2,1,0:T(8,128)(2,1)S(1)} all-to-all(bf16[64,32,128]{2,1,0:T(8,128)(2,1)S(1)} %shard_map.92), channel_id=1, replica_groups=mesh['z'=8,'y'=4,'c'=2,'x'=4] {'z'}, dimensions={0} | all-to-all | bytes 1048576 | tf_op jit(solution)/shard_map/all_to_all | solution.py:278
  214.1 5.2 %collective-permute-done.26.left = bf16[8,32,128]{2,1,0:T(8,128)(2,1)S(1)} collective-permute-done((bf16[8,32,128]{2,1,0:T(8,128)(2,1)S(1)}, bf16[8,32,128]{2,1,0:T(8,128)(2,1)S(1)}, u32[]{:S(2)}, u32[]{:S(2)}) %collective-permute-start.26) | collective-permute-done | bytes 65568 | tf_op jit(solution)/shard_map/ppermute | solution.py:37
  219.3 1.9 shard_map.94.own
  223.1 5.2 %collective-permute-done.28.left = bf16[8,32,128]{2,1,0:T(8,128)(2,1)S(1)} collective-permute-done((bf16[8,32,128]{2,1,0:T(8,128)(2,1)S(1)}, bf16[8,32,128]{2,1,0:T(8,128)(2,1)S(1)}, u32[]{:S(2)}, u32[]{:S(2)}) %collective-permute-start.28) | collective-permute-done | bytes 65568 | tf_op jit(solution)/shard_map/ppermute | solution.py:37
  228.3 1.9 shard_map.95.own
  232.1 5.2 %collective-permute-done.30.left = bf16[8,32,128]{2,1,0:T(8,128)(2,1)S(1)} collective-permute-done((bf16[8,32,128]{2,1,0:T(8,128)(2,1)S(1)}, bf16[8,32,128]{2,1,0:T(8,128)(2,1)S(1)}, u32[]{:S(2)}, u32[]{:S(2)}) %collective-permute-start.30) | collective-permute-done | bytes 65568 | tf_op jit(solution)/shard_map/ppermute | solution.py:37
  237.3 1.9 shard_map.96.refs_4_
  239.2 1.5 collective-permute-start.34
  240.7 3.0 %collective-permute-start.33 = (bf16[8,32,128]{2,1,0:T(8,128)(2,1)S(1)}, bf16[8,32,128]{2,1,0:T(8,128)(2,1)S(1)}, u32[]{:S(2)}, u32[]{:S(2)}) collective-permute-start(bf16[8,32,128]{2,1,0:T(8,128)(2,1)S(1)} %shard_map.96.refs_4_), channel_id=1, source_target_pairs={{0,2},{1,3},{2,0},{3,1},{4,6},{5,7},{6,4},{7,5},{8,10},{9,11},{10,... | collective-permute-start | bytes 196616 | tf_op jit(solution)/shard_map/ppermute | solution.py:37
  243.9 2.6 %collective-permute-done.33.refs_6_ = bf16[8,32,128]{2,1,0:T(8,128)(2,1)S(1)} collective-permute-done((bf16[8,32,128]{2,1,0:T(8,128)(2,1)S(1)}, bf16[8,32,128]{2,1,0:T(8,128)(2,1)S(1)}, u32[]{:S(2)}, u32[]{:S(2)}) %collective-permute-start.33) | collective-permute-done | bytes 65568 | tf_op jit(solution)/shard_map/ppermute | solution.py:37
  246.5 1.5 collective-permute-done.32.refs_5_
  (111 shorter events, 39.2 us)
Async XLA Ops:
  0.0 66.9 %copy-start = (bf16[2,1024,128]{2,1,0:T(8,128)(2,1)S(1)}, bf16[2,1024,128]{2,1,0:T(8,128)(2,1)}, u32[]{:S(2)}) copy-start(bf16[2,1024,128]{2,1,0:T(8,128)(2,1)} %param.8) | copy-start | bytes 1572868
  3.4 14.9 %all-to-all-start = ((s32[4,1,128]{2,1,0:T(1,128)}), s32[4,1,128]{2,1,0:T(1,128)S(1)}, u32[]{:S(2)}, u32[]{:S(2)}) async-start(s32[4,1,128]{2,1,0:T(1,128)} %broadcast_in_dim.37), calls=%async_computation | async-start | bytes 4096 | tf_op jit(solution)/shard_map/all_to_all | solution.py:278
  9.8 8.5 %collective-permute-start = (bf16[8,128,128]{2,1,0:T(8,128)(2,1)S(1)}, bf16[8,128,128]{2,1,0:T(8,128)(2,1)S(1)}, u32[]{:S(2)}, u32[]{:S(2)}) collective-permute-start(bf16[8,128,128]{2,1,0:T(8,128)(2,1)S(1)} %bitcast.72), channel_id=1, source_target_pairs={{0,1},{1,2},{2,3},{3,0},{4,5},{5,6},{6,7},{7,4},{8,9},{9,10},{10,1... | collective-permute-start | bytes 786440 | tf_op jit(solution)/shard_map/ppermute | solution.py:37
  11.1 7.1 %copy-start.3 = (bf16[4,1024,128]{2,1,0:T(8,128)(2,1)S(1)}, bf16[4,1024,128]{2,1,0:T(8,128)(2,1)}, u32[]{:S(2)}) copy-start(bf16[4,1024,128]{2,1,0:T(8,128)(2,1)} %param.9) | copy-start | bytes 3145732
  19.0 28.8 %all-to-all-start.1 = ((bf16[4,64,32,128]{3,2,1,0:T(8,128)(2,1)}), bf16[4,64,32,128]{3,2,1,0:T(8,128)(2,1)S(1)}, u32[]{:S(2)}, u32[]{:S(2)}) async-start(bf16[4,64,32,128]{3,2,1,0:T(8,128)(2,1)} %shard_map.82), calls=%async_computation.1 | async-start | bytes 4194304 | tf_op jit(solution)/shard_map/all_to_all | solution.py:278
  23.8 3.3 %copy-start.7 = (bf16[8,128,128]{2,1,0:T(8,128)(2,1)S(1)}, bf16[8,128,128]{2,1,0:T(8,128)(2,1)}, u32[]{:S(2)}) copy-start(bf16[8,128,128]{2,1,0:T(8,128)(2,1)} %copy-done.6) | copy-start | bytes 786436
  27.0 12.1 %collective-permute-start.1 = (s32[4,128]{1,0:T(4,128)S(1)}, s32[4,128]{1,0:T(4,128)S(1)}, u32[]{:S(2)}, u32[]{:S(2)}) collective-permute-start(s32[4,128]{1,0:T(4,128)S(1)} %bitcast.75), channel_id=1, source_target_pairs={{0,4},{4,0},{1,5},{5,1},{2,6},{6,2},{3,7},{7,3},{8,12},{12,8},{9,1... | collective-permute-start | bytes 6152 | tf_op jit(solution)/shard_map/ppermute | solution.py:37
  39.1 6.1 %collective-permute-start.4 = (s32[2,16]{1,0:T(2,128)S(1)}, s32[2,16]{1,0:T(2,128)S(1)}, u32[]{:S(2)}, u32[]{:S(2)}) collective-permute-start(s32[2,16]{1,0:T(2,128)S(1)} %bitcast.82), channel_id=1, source_target_pairs={{0,24},{8,0},{16,8},{24,16},{1,25},{9,1},{17,9},{25,17},{2,26},{10... | collective-permute-start | bytes 392 | tf_op jit(solution)/shard_map/ppermute | solution.py:37
  41.5 5.1 %collective-permute-start.3 = (s32[2,16]{1,0:T(2,128)S(1)}, s32[2,16]{1,0:T(2,128)S(1)}, u32[]{:S(2)}, u32[]{:S(2)}) collective-permute-start(s32[2,16]{1,0:T(2,128)S(1)} %bitcast.83), channel_id=1, source_target_pairs={{0,16},{8,24},{16,0},{24,8},{1,17},{9,25},{17,1},{25,9},{2,18},{10... | collective-permute-start | bytes 392 | tf_op jit(solution)/shard_map/ppermute | solution.py:37
  42.2 4.8 %collective-permute-start.2 = (s32[2,16]{1,0:T(2,128)S(1)}, s32[2,16]{1,0:T(2,128)S(1)}, u32[]{:S(2)}, u32[]{:S(2)}) collective-permute-start(s32[2,16]{1,0:T(2,128)S(1)} %bitcast.84), channel_id=1, source_target_pairs={{0,8},{8,16},{16,24},{24,0},{1,9},{9,17},{17,25},{25,1},{2,10},{10... | collective-permute-start | bytes 392 | tf_op jit(solution)/shard_map/ppermute | solution.py:37
  47.7 4.4 %copy-start.2 = (bf16[4,64,32,128]{3,2,1,0:T(8,128)(2,1)}, bf16[4,64,32,128]{3,2,1,0:T(8,128)(2,1)S(1)}, u32[]{:S(2)}) copy-start(bf16[4,64,32,128]{3,2,1,0:T(8,128)(2,1)S(1)} %all-to-all-done.1) | copy-start | bytes 6291460
  47.8 4.4 %collective-permute-start.5 = (bf16[256,32,128]{2,1,0:T(8,128)(2,1)S(1)}, bf16[256,32,128]{2,1,0:T(8,128)(2,1)}, u32[]{:S(2)}, u32[]{:S(2)}) collective-permute-start(bf16[256,32,128]{2,1,0:T(8,128)(2,1)S(1)} %bitcast.64), channel_id=1, source_target_pairs={{0,4},{4,0},{1,5},{5,1},{2,6},{6,2},{3,7},{7,3},{8,12},{12,8},{9,1... | collective-permute-start | bytes 6291464 | tf_op jit(solution)/shard_map/ppermute | solution.py:37
  58.5 8.1 %copy-start.4 = (bf16[64,32,128]{2,1,0:T(8,128)(2,1)S(1)}, bf16[64,32,128]{2,1,0:T(8,128)(2,1)}, u32[]{:S(2)}) copy-start(bf16[64,32,128]{2,1,0:T(8,128)(2,1)} %get-tuple-element.53.rest_0_) | copy-start | bytes 1572868
  58.5 8.1 %copy-start.9 = (s32[8,8]{1,0:T(8,128)S(1)}, s32[8,8]{1,0:T(8,128)}, u32[]{:S(2)}) copy-start(s32[8,8]{1,0:T(8,128)} %param.15) | copy-start | bytes 772
  58.6 8.2 %copy-start.8 = (bf16[8,128,128]{2,1,0:T(8,128)(2,1)S(1)}, bf16[8,128,128]{2,1,0:T(8,128)(2,1)}, u32[]{:S(2)}) copy-start(bf16[8,128,128]{2,1,0:T(8,128)(2,1)} %param.14) | copy-start | bytes 786436
  58.6 32.1 %all-to-all-start.2 = ((bf16[256,32,128]{2,1,0:T(8,128)(2,1)}), bf16[256,32,128]{2,1,0:T(8,128)(2,1)}, u32[]{:S(2)}, u32[]{:S(2)}) async-start(bf16[256,32,128]{2,1,0:T(8,128)(2,1)} %shard_map.84), calls=%async_computation.2 | async-start | bytes 4194304 | tf_op jit(solution)/shard_map/all_to_all | solution.py:278
  63.2 15.2 %collective-permute-start.6 = (bf16[64,32,128]{2,1,0:T(8,128)(2,1)}, bf16[64,32,128]{2,1,0:T(8,128)(2,1)}, u32[]{:S(2)}, u32[]{:S(2)}) collective-permute-start(bf16[64,32,128]{2,1,0:T(8,128)(2,1)} %get-tuple-element.47), channel_id=1, source_target_pairs={{0,1},{1,2},{2,3},{3,0},{4,5},{5,6},{6,7},{7,4},{8,9},{9,10},{10,1... | collective-permute-start | bytes 1572872 | tf_op jit(solution)/shard_map/ppermute | solution.py:37
  64.4 24.4 %collective-permute-start.7 = (bf16[64,32,128]{2,1,0:T(8,128)(2,1)}, bf16[64,32,128]{2,1,0:T(8,128)(2,1)}, u32[]{:S(2)}, u32[]{:S(2)}) collective-permute-start(bf16[64,32,128]{2,1,0:T(8,128)(2,1)} %get-tuple-element.48), channel_id=1, source_target_pairs={{0,2},{1,3},{2,0},{3,1},{4,6},{5,7},{6,4},{7,5},{8,10},{9,11},{10,... | collective-permute-start | bytes 1572872 | tf_op jit(solution)/shard_map/ppermute | solution.py:37
  65.3 25.4 %collective-permute-start.8 = (bf16[64,32,128]{2,1,0:T(8,128)(2,1)}, bf16[64,32,128]{2,1,0:T(8,128)(2,1)}, u32[]{:S(2)}, u32[]{:S(2)}) collective-permute-start(bf16[64,32,128]{2,1,0:T(8,128)(2,1)} %get-tuple-element.49), channel_id=1, source_target_pairs={{0,3},{1,0},{2,1},{3,2},{4,7},{5,4},{6,5},{7,6},{8,11},{9,8},{10,9... | collective-permute-start | bytes 1572872 | tf_op jit(solution)/shard_map/ppermute | solution.py:37
  66.7 24.0 %collective-permute-start.9 = (bf16[64,32,128]{2,1,0:T(8,128)(2,1)S(1)}, bf16[64,32,128]{2,1,0:T(8,128)(2,1)}, u32[]{:S(2)}, u32[]{:S(2)}) collective-permute-start(bf16[64,32,128]{2,1,0:T(8,128)(2,1)S(1)} %copy-done.4), channel_id=1, source_target_pairs={{0,4},{4,0},{1,5},{5,1},{2,6},{6,2},{3,7},{7,3},{8,12},{12,8},{9,1... | collective-permute-start | bytes 1572872 | tf_op jit(solution)/shard_map/ppermute | solution.py:37
  93.3 25.1 %all-to-all-start.3 = ((bf16[64,32,128]{2,1,0:T(8,128)(2,1)}), bf16[64,32,128]{2,1,0:T(8,128)(2,1)S(1)}, u32[]{:S(2)}, u32[]{:S(2)}) async-start(bf16[64,32,128]{2,1,0:T(8,128)(2,1)} %shard_map.85), calls=%async_computation.3 | async-start | bytes 1048576 | tf_op jit(solution)/shard_map/all_to_all | solution.py:278
  101.7 2.1 collective-permute-start.10
  101.7 3.0 %collective-permute-start.11 = (bf16[64,32,128]{2,1,0:T(8,128)(2,1)}, bf16[64,32,128]{2,1,0:T(8,128)(2,1)}, u32[]{:S(2)}, u32[]{:S(2)}) collective-permute-start(bf16[64,32,128]{2,1,0:T(8,128)(2,1)} %collective-permute-done.7.rest_2_), channel_id=1, source_target_pairs={{0,4},{4,0},{1,5},{5,1},{2,6},{6,2},{3,7},{7,3},{8,12},{12,8},{9,1... | collective-permute-start | bytes 1572872 | tf_op jit(solution)/shard_map/ppermute | solution.py:37
  102.2 3.2 %collective-permute-start.12 = (bf16[64,32,128]{2,1,0:T(8,128)(2,1)}, bf16[64,32,128]{2,1,0:T(8,128)(2,1)}, u32[]{:S(2)}, u32[]{:S(2)}) collective-permute-start(bf16[64,32,128]{2,1,0:T(8,128)(2,1)} %collective-permute-done.8.rest_3_), channel_id=1, source_target_pairs={{0,4},{4,0},{1,5},{5,1},{2,6},{6,2},{3,7},{7,3},{8,12},{12,8},{9,1... | collective-permute-start | bytes 1572872 | tf_op jit(solution)/shard_map/ppermute | solution.py:37
  103.9 1.6 copy-start.5
  118.6 2.0 collective-permute-start.14
  118.7 7.1 %collective-permute-start.13 = (bf16[8,32,128]{2,1,0:T(8,128)(2,1)S(1)}, bf16[8,32,128]{2,1,0:T(8,128)(2,1)S(1)}, u32[]{:S(2)}, u32[]{:S(2)}) collective-permute-start(bf16[8,32,128]{2,1,0:T(8,128)(2,1)S(1)} %get-tuple-element.59.own), channel_id=1, source_target_pairs={{0,4},{4,8},{8,12},{12,16},{16,20},{20,24},{24,28},{28,32},{32,36}... | collective-permute-start | bytes 196616 | tf_op jit(solution)/shard_map/ppermute | solution.py:37
  127.7 1.9 collective-permute-start.16
  127.7 7.1 %collective-permute-start.15 = (bf16[8,32,128]{2,1,0:T(8,128)(2,1)S(1)}, bf16[8,32,128]{2,1,0:T(8,128)(2,1)S(1)}, u32[]{:S(2)}, u32[]{:S(2)}) collective-permute-start(bf16[8,32,128]{2,1,0:T(8,128)(2,1)S(1)} %shard_map.88.own), channel_id=1, source_target_pairs={{0,4},{4,8},{8,12},{12,16},{16,20},{20,24},{24,28},{28,32},{32,36}... | collective-permute-start | bytes 196616 | tf_op jit(solution)/shard_map/ppermute | solution.py:37
  136.7 1.9 collective-permute-start.18
  136.7 7.1 %collective-permute-start.17 = (bf16[8,32,128]{2,1,0:T(8,128)(2,1)S(1)}, bf16[8,32,128]{2,1,0:T(8,128)(2,1)S(1)}, u32[]{:S(2)}, u32[]{:S(2)}) collective-permute-start(bf16[8,32,128]{2,1,0:T(8,128)(2,1)S(1)} %shard_map.89.own), channel_id=1, source_target_pairs={{0,4},{4,8},{8,12},{12,16},{16,20},{20,24},{24,28},{28,32},{32,36}... | collective-permute-start | bytes 196616 | tf_op jit(solution)/shard_map/ppermute | solution.py:37
  145.7 26.5 %all-to-all-start.4 = ((bf16[256,32,128]{2,1,0:T(8,128)(2,1)}), bf16[256,32,128]{2,1,0:T(8,128)(2,1)}, u32[]{:S(2)}, u32[]{:S(2)}) async-start(bf16[256,32,128]{2,1,0:T(8,128)(2,1)} %shard_map.86), calls=%async_computation.4 | async-start | bytes 4194304 | tf_op jit(solution)/shard_map/all_to_all | solution.py:278
  150.2 4.7 %collective-permute-start.21 = (bf16[8,32,128]{2,1,0:T(8,128)(2,1)S(1)}, bf16[8,32,128]{2,1,0:T(8,128)(2,1)S(1)}, u32[]{:S(2)}, u32[]{:S(2)}) collective-permute-start(bf16[8,32,128]{2,1,0:T(8,128)(2,1)S(1)} %shard_map.90.rest_0_.refs_0_), channel_id=1, source_target_pairs={{0,3},{1,0},{2,1},{3,2},{4,7},{5,4},{6,5},{7,6},{8,11},{9,8},{10,9... | collective-permute-start | bytes 196616 | tf_op jit(solution)/shard_map/ppermute | solution.py:37
  151.8 5.8 %collective-permute-start.20 = (bf16[8,32,128]{2,1,0:T(8,128)(2,1)S(1)}, bf16[8,32,128]{2,1,0:T(8,128)(2,1)S(1)}, u32[]{:S(2)}, u32[]{:S(2)}) collective-permute-start(bf16[8,32,128]{2,1,0:T(8,128)(2,1)S(1)} %shard_map.90.rest_0_.refs_0_), channel_id=1, source_target_pairs={{0,2},{1,3},{2,0},{3,1},{4,6},{5,7},{6,4},{7,5},{8,10},{9,11},{10,... | collective-permute-start | bytes 196616 | tf_op jit(solution)/shard_map/ppermute | solution.py:37
  154.7 4.3 %collective-permute-start.19 = (bf16[8,32,128]{2,1,0:T(8,128)(2,1)S(1)}, bf16[8,32,128]{2,1,0:T(8,128)(2,1)S(1)}, u32[]{:S(2)}, u32[]{:S(2)}) collective-permute-start(bf16[8,32,128]{2,1,0:T(8,128)(2,1)S(1)} %shard_map.90.rest_0_.refs_0_), channel_id=1, source_target_pairs={{0,1},{1,2},{2,3},{3,0},{4,5},{5,6},{6,7},{7,4},{8,9},{9,10},{10,1... | collective-permute-start | bytes 196616 | tf_op jit(solution)/shard_map/ppermute | solution.py:37
  162.5 5.3 %collective-permute-start.22 = (bf16[16,32,128]{2,1,0:T(8,128)(2,1)}, bf16[16,32,128]{2,1,0:T(8,128)(2,1)}, u32[]{:S(2)}, u32[]{:S(2)}) collective-permute-start(bf16[16,32,128]{2,1,0:T(8,128)(2,1)} %get-tuple-element.63), channel_id=1, source_target_pairs={{0,1},{1,2},{2,3},{3,0},{4,5},{5,6},{6,7},{7,4},{8,9},{9,10},{10,1... | collective-permute-start | bytes 393224 | tf_op jit(solution)/shard_map/ppermute | solution.py:37
  163.2 6.8 %collective-permute-start.23 = (bf16[16,32,128]{2,1,0:T(8,128)(2,1)}, bf16[16,32,128]{2,1,0:T(8,128)(2,1)}, u32[]{:S(2)}, u32[]{:S(2)}) collective-permute-start(bf16[16,32,128]{2,1,0:T(8,128)(2,1)} %get-tuple-element.64), channel_id=1, source_target_pairs={{0,2},{1,3},{2,0},{3,1},{4,6},{5,7},{6,4},{7,5},{8,10},{9,11},{10,... | collective-permute-start | bytes 393224 | tf_op jit(solution)/shard_map/ppermute | solution.py:37
  164.7 6.5 %collective-permute-start.24 = (bf16[16,32,128]{2,1,0:T(8,128)(2,1)S(1)}, bf16[16,32,128]{2,1,0:T(8,128)(2,1)}, u32[]{:S(2)}, u32[]{:S(2)}) collective-permute-start(bf16[16,32,128]{2,1,0:T(8,128)(2,1)S(1)} %get-tuple-element.65), channel_id=1, source_target_pairs={{0,3},{1,0},{2,1},{3,2},{4,7},{5,4},{6,5},{7,6},{8,11},{9,8},{10,9... | collective-permute-start | bytes 393224 | tf_op jit(solution)/shard_map/ppermute | solution.py:37
  184.8 1.9 collective-permute-start.25
  212.1 2.0 collective-permute-start.27
  212.2 7.1 %collective-permute-start.26 = (bf16[8,32,128]{2,1,0:T(8,128)(2,1)S(1)}, bf16[8,32,128]{2,1,0:T(8,128)(2,1)S(1)}, u32[]{:S(2)}, u32[]{:S(2)}) collective-permute-start(bf16[8,32,128]{2,1,0:T(8,128)(2,1)S(1)} %get-tuple-element.67.own), channel_id=1, source_target_pairs={{0,4},{4,8},{8,12},{12,16},{16,20},{20,24},{24,28},{28,32},{32,36}... | collective-permute-start | bytes 196616 | tf_op jit(solution)/shard_map/ppermute | solution.py:37
  221.2 1.9 collective-permute-start.29
  221.2 7.1 %collective-permute-start.28 = (bf16[8,32,128]{2,1,0:T(8,128)(2,1)S(1)}, bf16[8,32,128]{2,1,0:T(8,128)(2,1)S(1)}, u32[]{:S(2)}, u32[]{:S(2)}) collective-permute-start(bf16[8,32,128]{2,1,0:T(8,128)(2,1)S(1)} %shard_map.94.own), channel_id=1, source_target_pairs={{0,4},{4,8},{8,12},{12,16},{16,20},{20,24},{24,28},{28,32},{32,36}... | collective-permute-start | bytes 196616 | tf_op jit(solution)/shard_map/ppermute | solution.py:37
  230.2 1.9 collective-permute-start.31
  230.2 7.1 %collective-permute-start.30 = (bf16[8,32,128]{2,1,0:T(8,128)(2,1)S(1)}, bf16[8,32,128]{2,1,0:T(8,128)(2,1)S(1)}, u32[]{:S(2)}, u32[]{:S(2)}) collective-permute-start(bf16[8,32,128]{2,1,0:T(8,128)(2,1)S(1)} %shard_map.95.own), channel_id=1, source_target_pairs={{0,4},{4,8},{8,12},{12,16},{16,20},{20,24},{24,28},{28,32},{32,36}... | collective-permute-start | bytes 196616 | tf_op jit(solution)/shard_map/ppermute | solution.py:37
  239.2 4.7 %collective-permute-start.34 = (bf16[8,32,128]{2,1,0:T(8,128)(2,1)S(1)}, bf16[8,32,128]{2,1,0:T(8,128)(2,1)S(1)}, u32[]{:S(2)}, u32[]{:S(2)}) collective-permute-start(bf16[8,32,128]{2,1,0:T(8,128)(2,1)S(1)} %shard_map.96.refs_4_), channel_id=1, source_target_pairs={{0,3},{1,0},{2,1},{3,2},{4,7},{5,4},{6,5},{7,6},{8,11},{9,8},{10,9... | collective-permute-start | bytes 196616 | tf_op jit(solution)/shard_map/ppermute | solution.py:37
  240.7 5.8 %collective-permute-start.33 = (bf16[8,32,128]{2,1,0:T(8,128)(2,1)S(1)}, bf16[8,32,128]{2,1,0:T(8,128)(2,1)S(1)}, u32[]{:S(2)}, u32[]{:S(2)}) collective-permute-start(bf16[8,32,128]{2,1,0:T(8,128)(2,1)S(1)} %shard_map.96.refs_4_), channel_id=1, source_target_pairs={{0,2},{1,3},{2,0},{3,1},{4,6},{5,7},{6,4},{7,5},{8,10},{9,11},{10,... | collective-permute-start | bytes 196616 | tf_op jit(solution)/shard_map/ppermute | solution.py:37
  243.8 4.3 %collective-permute-start.32 = (bf16[8,32,128]{2,1,0:T(8,128)(2,1)S(1)}, bf16[8,32,128]{2,1,0:T(8,128)(2,1)S(1)}, u32[]{:S(2)}, u32[]{:S(2)}) collective-permute-start(bf16[8,32,128]{2,1,0:T(8,128)(2,1)S(1)} %shard_map.96.refs_4_), channel_id=1, source_target_pairs={{0,1},{1,2},{2,3},{3,0},{4,5},{5,6},{6,7},{7,4},{8,9},{9,10},{10,1... | collective-permute-start | bytes 196616 | tf_op jit(solution)/shard_map/ppermute | solution.py:37
  (2 other events, 2.3 us)

commit v2 on v1

--- a/solution.py
+++ b/solution.py
@@ -80,39 +80,31 @@
 
 
 def place_kernel(count, places_ref, *rest):
-    ins, (out_ref, held, dense, sems) = rest[:count], rest[count:]
-    per = held.shape[1]
-    arriving = [pltpu.make_async_copy(ins[n], held.at[n], sems.at[n]) for n in range(count)]
-    for copy in arriving:
-        copy.start()
+    ins, (out_ref, dense, sem) = rest[:count], rest[count:]
+    per = ins[0].shape[0]
     dense[...] = jnp.zeros_like(dense)
-    for n in range(count):
-        arriving[n].wait()
-
-        def body(p, carry, n=n):
+    for n, values in enumerate(ins):
+
+        def body(p, carry, n=n, values=values):
             at = places_ref[n * per + p]
-            dense[at] = dense[at] + held[n, p]
+            dense[at] = dense[at] + values[p]
             return carry
 
         lax.fori_loop(0, per, body, 0, unroll=8)
-    leaving = pltpu.make_async_copy(dense.at[pl.ds(0, 256)], out_ref, sems.at[count])
-    leaving.start()
-    leaving.wait()
+    copy = pltpu.make_async_copy(dense.at[pl.ds(0, 256)], out_ref, sem)
+    copy.start()
+    copy.wait()
 
 
 def place(places, buffers):
-    count, per = len(buffers), buffers[0].shape[0]
+    count = len(buffers)
     return pl.pallas_call(
         functools.partial(place_kernel, count),
-        in_specs=[SM] + [ANY] * count,
+        in_specs=[SM] + [VM] * count,
         out_specs=ANY,
         out_shape=shape(256, RW, B),
-        scratch_shapes=[
-            pltpu.VMEM((count, per, RW, B), BF),
-            pltpu.VMEM((257, RW, B), BF),
-            pltpu.SemaphoreType.DMA((count + 1,)),
-        ],
-        compiler_params=params(60),
+        scratch_shapes=[pltpu.VMEM((257, RW, B), BF), pltpu.SemaphoreType.DMA],
+        compiler_params=params(),
         cost_estimate=cost(1, 1),
     )(places, *buffers)
 
@@ -195,7 +187,7 @@
     )(pieces, incident, inverse)
 
 
-def sweep_kernel(ids_ref, left, own, right, drive_ref, near_ref, inverse, out_ref, held):
+def sweep_kernel(ids_ref, right, own, left, drive_ref, near_ref, inverse, out_ref, held):
     held[0:BLKS] = left[...]
     held[BLKS : 2 * BLKS] = own[...]
     held[2 * BLKS : 3 * BLKS] = right[...]
@@ -206,7 +198,7 @@
         out_ref[g] = jnp.dot(rest, inverse[g], preferred_element_type=F32).astype(BF)
 
 
-def sweep(ids, left, own, right, drive, near, inverse):
+def sweep(ids, right, own, left, drive, near, inverse):
     return pl.pallas_call(
         sweep_kernel,
         in_specs=[SM] + [VM] * 6,
@@ -215,7 +207,7 @@
         scratch_shapes=[pltpu.VMEM((3 * BLKS, RW, B), BF)],
         compiler_params=params(),
         cost_estimate=cost(1, 1),
-    )(ids, left, own, right, drive, near, inverse)
+    )(ids, right, own, left, drive, near, inverse)
 
 
 def gather_waves(x, pieces, whole):
@@ -228,7 +220,7 @@
     pieces, coupling, outs, whole = rest[:4], rest[4], rest[5:9], rest[9]
     gather_waves(x_ref[0], pieces, whole)
     for j in range(16):
-        gathered = jnp.concatenate([whole[src_ref[i * 16 + j]] for i in range(4)], axis=1)
+        gathered = jnp.concatenate([whole[src_ref[0, 0, i, j]] for i in range(4)], axis=1)
         parcel = jnp.dot(gathered, coupling[j], preferred_element_type=F32).astype(BF)
         for n in range(NX):
             outs[n][j] = parcel[n * RW : (n + 1) * RW]
@@ -285,8 +277,8 @@
     past = history.reshape(4, BLKS, B, B)
     coupling = inter[:, 0]
 
-    meta = jnp.concatenate([dest_blocks[:, 0].reshape(64), src_lists[0, 0].T.reshape(64)])
-    metas = exchange(jnp.broadcast_to(meta[None], (NX, 128)), "x")
+    lists = jnp.broadcast_to(dest_blocks[:, 0][None], (NX, 4, 16))
+    metas = exchange(lists, "x")
 
     older = shift(past[3], "x", 1)
     sources = src_lists.swapaxes(2, 3)
@@ -297,11 +289,9 @@
     later_past = jnp.concatenate([older[None], past[:3]], 0)
     later_sent = parcels(x_scalar, sources, later_past, coupling, True)
 
-    metas = after(metas, sent)
-    metas = jnp.stack([metas, shift(metas, "c", 1)])
-    late_sources = metas[0, 0, 64:]
-    targets = metas[:, :, :64]
-    late_targets = jnp.stack(spread(metas[:, 0, :16], "y"), axis=1)
+    metas = after(metas, sent).reshape(NX, 64)
+    targets = jnp.stack([metas, shift(metas, "c", 1)])
+    late_targets = jnp.stack(spread(targets[:, 0, :16], "y"), axis=1)
     late_targets = jnp.take(late_targets, (y - jnp.arange(NY)) % NY, axis=1)
 
     def place_of(target):
@@ -315,7 +305,7 @@
     late_places = jnp.where(same & (across == y), inner, 64).reshape(128)
 
     by_distance = places.reshape(2, NX, 64)[:, (x - jnp.arange(NX)) % NX].reshape(512)
-    newest = after(coupling[0], sent).swapaxes(2, 3).reshape(16, 4 * B, B)
+    newest = after(coupling, sent)[0].swapaxes(2, 3).reshape(16, 4 * B, B)
     crossed = after(crossed, later_sent, places, by_distance, late_places, newest)
     crossed = crossed.reshape(256, RW, B)
     dense = place(places, [crossed, shift(crossed, "c", 1)])
@@ -336,12 +326,12 @@
     def one_sweep(current, drive):
         right = shift(current, BLK, -1)
         left = shift(current, BLK, 1)
-        return sweep(ids, left, current, right, drive, near_t, inverse_t)
+        return sweep(ids, right, current, left, drive, near_t, inverse_t)
 
     later_own = shift(later_crossed[0], "c", 1)
     later_crossed = after(later_crossed, near_t, inverse_t, incident, ids, later_own)
 
-    halves = after(halves, later_crossed)
+    halves = after(halves, near_t, inverse_t, incident, ids)
     summed = add(halves)
     pieces = exchange(summed, "z")
 
@@ -355,7 +345,7 @@
     later_halves = exchange(after(later_dense, current), "y")
     outputs = spread(current, "x")
 
-    late = late_parcels(x_scalar, late_sources, outputs, newest)
+    late = late_parcels(x_scalar, sources, outputs, newest)
     late = [late[0], shift(late[1], "x", 1), shift(late[2], "x", 2), shift(late[3], "x", -1)]
     mine = late[3]
     for n in range(NX - 2, -1, -1):

time: 250 us -> 246 us (0.984)
  the two profiles are of different devices: /device:TPU:4 before, /device:TPU:6 now
where the time goes in v2:
time: 246 us; the launch traced here: 245 us
  waiting for transfers between devices  94.6 us (38%)
  starting transfers between devices  48.3 us (20%)
  Pallas kernels  43.5 us (18%)
  blocking collectives  33.5 us (14%)
  local copies, waits for them, and re-layouts  21.4 us (9%)
  other arithmetic  3.29 us (1%)
    ppermute x35, waiting for transfers between devices, shift(): lax.ppermute(value, axis, [(i, (i + distance) % count) for i in range(cou...  68.1 us
    all_to_all x2, blocking collectives, exchange(): return lax.all_to_all(value, axis, split_axis=0, concat_axis=0, tiled=True)  33.5 us
    all_to_all x5, starting transfers between devices, exchange(): return lax.all_to_all(value, axis, split_axis=0, concat_axis=0, tiled=True)  29 us
    all_to_all x5, waiting for transfers between devices, exchange(): return lax.all_to_all(value, axis, split_axis=0, concat_axis=0, tiled=True)  26.6 us
    ppermute x35, starting transfers between devices, shift(): lax.ppermute(value, axis, [(i, (i + distance) % count) for i in range(cou...  19.3 us
    pallas_call x2, Pallas kernels, parcels(): pl.pallas_call(parcels_kernel, grid=(4,), in_specs=[SM, SM, pl.BlockSpec(...  14.1 us
    pallas_call x6, Pallas kernels, sweep(): pl.pallas_call(sweep_kernel, in_specs=[SM] + [VM] * 6, out_specs=VM, out_...  11.5 us
    pallas_call x2, Pallas kernels, place(): pl.pallas_call(functools.partial(place_kernel, count), in_specs=[SM] + [V...  8.58 us
  transfers between devices with their start and end apart: 40, of which 30 were waited for; matrix products, arithmetic and copies ran while one was open for 7% of the time, Pallas kernels for 10%

profile of v2, /device:TPU:6, one launch (start us, length us, event | category | flops | bytes accessed | tf_op | source)
XLA Modules:
  0.0 245.1 jit_solution(493889274757224472)
XLA Ops:
  1.3 5.4 %all-to-all-start = ((s32[4,4,16]{2,1,0:T(4,128)}), s32[4,4,16]{2,1,0:T(4,128)S(1)}, u32[]{:S(2)}, u32[]{:S(2)}) async-start(s32[4,4,16]{2,1,0:T(4,128)} %broadcast_in_dim.41), calls=%async_computation | async-start | bytes 16384 | tf_op jit(solution)/shard_map/all_to_all | solution.py:270
  8.0 7.1 %shard_map.82 = bf16[4,64,32,128]{3,2,1,0:T(8,128)(2,1)} custom-call(s32[1]{0:T(128)} %bitcast.first_ref.x_ref, s32[4,1,4,16]{3,2,1,0:T(4,128)} %bitcast.56, bf16[4,8,128,128]{3,2,1,0:T(8,128)(2,1)} %bitcast.62, bf16[4,16,4,128,128]{4,3,2,1,0:T(8,128)(2,1)} %bitcast.59), custom_call_target="tpu_custom_call" | custom-call | flops 1 | bytes 1 | tf_op jit(solution)/shard_map/pallas_call | solution.py:65
  15.8 5.9 %all-to-all-start.1 = ((bf16[4,64,32,128]{3,2,1,0:T(8,128)(2,1)}), bf16[4,64,32,128]{3,2,1,0:T(8,128)(2,1)S(1)}, u32[]{:S(2)}, u32[]{:S(2)}) async-start(bf16[4,64,32,128]{3,2,1,0:T(8,128)(2,1)} %shard_map.82), calls=%async_computation.1 | async-start | bytes 4194304 | tf_op jit(solution)/shard_map/all_to_all | solution.py:270
  24.0 3.2 %slice_bitcast_fusion = bf16[16,4,128,128]{2,3,1,0:T(8,128)(2,1)} fusion(bf16[4,16,4,128,128]{4,3,2,1,0:T(8,128)(2,1)} %bitcast.60), kind=kLoop, calls=%fused_computation.2 | loop fusion | bytes 4194304 | tf_op jit(solution)/shard_map/transpose | solution.py:308
  27.2 7.1 %shard_map.83 = (bf16[64,32,128]{2,1,0:T(8,128)(2,1)}, bf16[64,32,128]{2,1,0:T(8,128)(2,1)}, bf16[64,32,128]{2,1,0:T(8,128)(2,1)}, bf16[64,32,128]{2,1,0:T(8,128)(2,1)}) custom-call(s32[1]{0:T(128)} %bitcast.first_ref.x_ref, s32[4,1,4,16]{3,2,1,0:T(4,128)} %bitcast.57, bf16[4,8,128,128]{3,2,1,0:T(8,128)(2,1)} %pad_maximum_fusion.past_ref, ...), custom_call_target="tpu_custom_call" | custom-call | flops 1 | bytes 1 | tf_op jit(solution)/shard_map/pallas_call | solution.py:65
  34.3 3.9 %copy.16 = bf16[16,4,128,128]{3,2,1,0:T(8,128)(2,1)} copy(bf16[16,4,128,128]{2,3,1,0:T(8,128)(2,1)} %slice_bitcast_fusion) | data formatting | bytes 4194304 | tf_op jit(solution)/shard_map/transpose | solution.py:308
  38.2 2.4 collective-permute-start.4
  43.1 2.6 %collective-permute-done.3 = s32[2,16]{1,0:T(2,128)S(1)} collective-permute-done((s32[2,16]{1,0:T(2,128)S(1)}, s32[2,16]{1,0:T(2,128)S(1)}, u32[]{:S(2)}, u32[]{:S(2)}) %collective-permute-start.3) | collective-permute-done | bytes 160 | tf_op jit(solution)/shard_map/ppermute | solution.py:37
  47.0 4.1 %collective-permute-done.5.rest_1_ = bf16[256,32,128]{2,1,0:T(8,128)(2,1)S(1)} collective-permute-done((bf16[256,32,128]{2,1,0:T(8,128)(2,1)S(1)}, bf16[256,32,128]{2,1,0:T(8,128)(2,1)S(1)}, u32[]{:S(2)}, u32[]{:S(2)}) %collective-permute-start.5) | collective-permute-done | bytes 2097184 | tf_op jit(solution)/shard_map/ppermute | solution.py:37
  51.1 3.7 %shard_map.84 = bf16[256,32,128]{2,1,0:T(8,128)(2,1)S(1)} custom-call(s32[512]{0:T(512)S(1)} %fusion.6.places_ref, bf16[256,32,128]{2,1,0:T(8,128)(2,1)S(1)} %bitcast.55, bf16[256,32,128]{2,1,0:T(8,128)(2,1)S(1)} %collective-permute-done.5.rest_1_), custom_call_target="tpu_custom_call" | custom-call | flops 1 | bytes 1 | tf_op jit(solution)/shard_map/pallas_call | solution.py:101
  56.2 4.6 %all-to-all-start.2 = ((bf16[256,32,128]{2,1,0:T(8,128)(2,1)}), bf16[256,32,128]{2,1,0:T(8,128)(2,1)}, u32[]{:S(2)}, u32[]{:S(2)}) async-start(bf16[256,32,128]{2,1,0:T(8,128)(2,1)} %copy-done.3), calls=%async_computation.2 | async-start | bytes 4194304 | tf_op jit(solution)/shard_map/all_to_all | solution.py:270
  60.9 2.9 %collective-permute-start.7 = (bf16[64,32,128]{2,1,0:T(8,128)(2,1)}, bf16[64,32,128]{2,1,0:T(8,128)(2,1)}, u32[]{:S(2)}, u32[]{:S(2)}) collective-permute-start(bf16[64,32,128]{2,1,0:T(8,128)(2,1)} %get-tuple-element.52), channel_id=1, source_target_pairs={{0,2},{1,3},{2,0},{3,1},{4,6},{5,7},{6,4},{7,5},{8,10},{9,11},{10,... | collective-permute-start | bytes 1572872 | tf_op jit(solution)/shard_map/ppermute | solution.py:37
  63.9 3.1 %copy.17 = bf16[8,8,128,128]{3,2,1,0:T(8,128)(2,1)S(1)} copy(bf16[8,8,128,128]{2,3,1,0:T(8,128)(2,1)} %bitcast.65) | data formatting | bytes 4194304 | tf_op jit(solution)/shard_map/transpose | solution.py:320
  68.3 19.6 %all-to-all-done.2.halves = bf16[256,32,128]{2,1,0:T(8,128)(2,1)} async-done(((bf16[256,32,128]{2,1,0:T(8,128)(2,1)}), bf16[256,32,128]{2,1,0:T(8,128)(2,1)}, u32[]{:S(2)}, u32[]{:S(2)}) %all-to-all-start.2) | async-done | bytes 2097184 | tf_op jit(solution)/shard_map/all_to_all | solution.py:270
  87.9 2.6 %shard_map.85 = bf16[64,32,128]{2,1,0:T(8,128)(2,1)} custom-call(bf16[256,32,128]{2,1,0:T(8,128)(2,1)} %all-to-all-done.2.halves), custom_call_target="tpu_custom_call" | custom-call | flops 1 | bytes 1 | tf_op jit(solution)/shard_map/pallas_call | solution.py:121
  90.5 8.4 %all-to-all-start.3 = ((bf16[64,32,128]{2,1,0:T(8,128)(2,1)}), bf16[64,32,128]{2,1,0:T(8,128)(2,1)S(1)}, u32[]{:S(2)}, u32[]{:S(2)}) async-start(bf16[64,32,128]{2,1,0:T(8,128)(2,1)} %shard_map.85), calls=%async_computation.3 | async-start | bytes 1048576 | tf_op jit(solution)/shard_map/all_to_all | solution.py:270
  102.7 4.8 %shard_map.86 = bf16[256,32,128]{2,1,0:T(8,128)(2,1)S(1)} custom-call(s32[512]{0:T(512)S(1)} %reshape.152.places_ref, bf16[64,32,128]{2,1,0:T(8,128)(2,1)} %get-tuple-element.54.rest_0_, bf16[64,32,128]{2,1,0:T(8,128)(2,1)} %collective-permute-done.6.rest_1_, bf16[64,32,128]{2,1,0:T(8,128)(2,1)} %collective-permute-done.7.rest_2_, ...), custom_call_target="tpu_custom_call" | custom-call | flops 1 | bytes 1 | tf_op jit(solution)/shard_map/pallas_call | solution.py:101
  108.9 7.0 %all-to-all-done.3.pieces = bf16[64,32,128]{2,1,0:T(8,128)(2,1)S(1)} async-done(((bf16[64,32,128]{2,1,0:T(8,128)(2,1)}), bf16[64,32,128]{2,1,0:T(8,128)(2,1)S(1)}, u32[]{:S(2)}, u32[]{:S(2)}) %all-to-all-start.3) | async-done | bytes 524320 | tf_op jit(solution)/shard_map/all_to_all | solution.py:270
  116.7 1.4 collective-permute-done.13.right
  118.1 5.2 %collective-permute-done.14.left = bf16[8,32,128]{2,1,0:T(8,128)(2,1)S(1)} collective-permute-done((bf16[8,32,128]{2,1,0:T(8,128)(2,1)S(1)}, bf16[8,32,128]{2,1,0:T(8,128)(2,1)S(1)}, u32[]{:S(2)}, u32[]{:S(2)}) %collective-permute-start.14) | collective-permute-done | bytes 65568 | tf_op jit(solution)/shard_map/ppermute | solution.py:37
  123.3 1.9 shard_map.88.own
  125.7 1.4 collective-permute-done.15.right
  127.1 5.2 %collective-permute-done.16.left = bf16[8,32,128]{2,1,0:T(8,128)(2,1)S(1)} collective-permute-done((bf16[8,32,128]{2,1,0:T(8,128)(2,1)S(1)}, bf16[8,32,128]{2,1,0:T(8,128)(2,1)S(1)}, u32[]{:S(2)}, u32[]{:S(2)}) %collective-permute-start.16) | collective-permute-done | bytes 65568 | tf_op jit(solution)/shard_map/ppermute | solution.py:37
  132.3 1.9 shard_map.89.own
  136.1 5.2 %collective-permute-done.18.left = bf16[8,32,128]{2,1,0:T(8,128)(2,1)S(1)} collective-permute-done((bf16[8,32,128]{2,1,0:T(8,128)(2,1)S(1)}, bf16[8,32,128]{2,1,0:T(8,128)(2,1)S(1)}, u32[]{:S(2)}, u32[]{:S(2)}) %collective-permute-start.18) | collective-permute-done | bytes 65568 | tf_op jit(solution)/shard_map/ppermute | solution.py:37
  141.3 1.9 shard_map.90.rest_0_.refs_0_
  143.2 4.6 %all-to-all-start.4 = ((bf16[256,32,128]{2,1,0:T(8,128)(2,1)}), bf16[256,32,128]{2,1,0:T(8,128)(2,1)}, u32[]{:S(2)}, u32[]{:S(2)}) async-start(bf16[256,32,128]{2,1,0:T(8,128)(2,1)} %copy-done.2), calls=%async_computation.4 | async-start | bytes 4194304 | tf_op jit(solution)/shard_map/all_to_all | solution.py:270
  147.9 2.9 %collective-permute-start.20 = (bf16[8,32,128]{2,1,0:T(8,128)(2,1)S(1)}, bf16[8,32,128]{2,1,0:T(8,128)(2,1)S(1)}, u32[]{:S(2)}, u32[]{:S(2)}) collective-permute-start(bf16[8,32,128]{2,1,0:T(8,128)(2,1)S(1)} %shard_map.90.rest_0_.refs_0_), channel_id=1, source_target_pairs={{0,2},{1,3},{2,0},{3,1},{4,6},{5,7},{6,4},{7,5},{8,10},{9,11},{10,... | collective-permute-start | bytes 196616 | tf_op jit(solution)/shard_map/ppermute | solution.py:37
  152.1 1.6 collective-permute-done.20.rest_2_.refs_2_
  153.7 2.5 %collective-permute-done.21.rest_3_.refs_3_ = bf16[8,32,128]{2,1,0:T(8,128)(2,1)S(1)} collective-permute-done((bf16[8,32,128]{2,1,0:T(8,128)(2,1)S(1)}, bf16[8,32,128]{2,1,0:T(8,128)(2,1)S(1)}, u32[]{:S(2)}, u32[]{:S(2)}) %collective-permute-start.21) | collective-permute-done | bytes 65568 | tf_op jit(solution)/shard_map/ppermute | solution.py:37
  156.3 1.6 copy-done.1
  157.9 2.1 shard_map.91
  162.0 3.1 %collective-permute-done.22 = bf16[16,32,128]{2,1,0:T(8,128)(2,1)S(1)} collective-permute-done((bf16[16,32,128]{2,1,0:T(8,128)(2,1)}, bf16[16,32,128]{2,1,0:T(8,128)(2,1)S(1)}, u32[]{:S(2)}, u32[]{:S(2)}) %collective-permute-start.22) | collective-permute-done | bytes 131104 | tf_op jit(solution)/shard_map/ppermute | solution.py:37
  165.1 2.3 collective-permute-done.23
  169.8 12.6 %all_to_all.35.first = bf16[64,32,128]{2,1,0:T(8,128)(2,1)S(1)} all-to-all(bf16[64,32,128]{2,1,0:T(8,128)(2,1)S(1)} %bitcast.64), channel_id=1, replica_groups=mesh['z'=8,'y'=4,'c'=2,'x'=4] {'y'}, dimensions={0} | all-to-all | bytes 1048576 | tf_op jit(solution)/shard_map/all_to_all | solution.py:270
  182.3 1.9 collective-permute-done.25.second
  184.2 3.2 %shard_map.92 = bf16[64,32,128]{2,1,0:T(8,128)(2,1)S(1)} custom-call(s32[128]{0:T(128)S(1)} %and_select_fusion.8.places_ref, bf16[256,32,128]{2,1,0:T(8,128)(2,1)} %all-to-all-done.4.halves, bf16[64,32,128]{2,1,0:T(8,128)(2,1)S(1)} %all_to_all.35.first, bf16[64,32,128]{2,1,0:T(8,128)(2,1)S(1)} %collective-permute-done.25.second), custom_call_target="tpu_custom_call" | custom-call | flops 1 | bytes 1 | tf_op jit(solution)/shard_map/pallas_call | solution.py:153
  187.4 21.0 %all_to_all.36.pieces = bf16[64,32,128]{2,1,0:T(8,128)(2,1)S(1)} all-to-all(bf16[64,32,128]{2,1,0:T(8,128)(2,1)S(1)} %shard_map.92), channel_id=1, replica_groups=mesh['z'=8,'y'=4,'c'=2,'x'=4] {'z'}, dimensions={0} | all-to-all | bytes 1048576 | tf_op jit(solution)/shard_map/all_to_all | solution.py:270
  209.1 1.4 collective-permute-done.26.right
  210.5 5.2 %collective-permute-done.27.left = bf16[8,32,128]{2,1,0:T(8,128)(2,1)S(1)} collective-permute-done((bf16[8,32,128]{2,1,0:T(8,128)(2,1)S(1)}, bf16[8,32,128]{2,1,0:T(8,128)(2,1)S(1)}, u32[]{:S(2)}, u32[]{:S(2)}) %collective-permute-start.27) | collective-permute-done | bytes 65568 | tf_op jit(solution)/shard_map/ppermute | solution.py:37
  215.7 1.9 shard_map.94.own
  219.6 5.2 %collective-permute-done.29.left = bf16[8,32,128]{2,1,0:T(8,128)(2,1)S(1)} collective-permute-done((bf16[8,32,128]{2,1,0:T(8,128)(2,1)S(1)}, bf16[8,32,128]{2,1,0:T(8,128)(2,1)S(1)}, u32[]{:S(2)}, u32[]{:S(2)}) %collective-permute-start.29) | collective-permute-done | bytes 65568 | tf_op jit(solution)/shard_map/ppermute | solution.py:37
  224.7 1.9 shard_map.95.own
  228.6 5.2 %collective-permute-done.31.left = bf16[8,32,128]{2,1,0:T(8,128)(2,1)S(1)} collective-permute-done((bf16[8,32,128]{2,1,0:T(8,128)(2,1)S(1)}, bf16[8,32,128]{2,1,0:T(8,128)(2,1)S(1)}, u32[]{:S(2)}, u32[]{:S(2)}) %collective-permute-start.31) | collective-permute-done | bytes 65568 | tf_op jit(solution)/shard_map/ppermute | solution.py:37
  233.7 1.9 shard_map.96.refs_4_
  236.4 2.2 collective-permute-start.33
  239.9 2.2 collective-permute-done.33.refs_6_
  242.2 1.9 collective-permute-done.34.refs_7_
  (107 shorter events, 33.8 us)
Async XLA Ops:
  0.0 67.2 %copy-start = (bf16[2,1024,128]{2,1,0:T(8,128)(2,1)S(1)}, bf16[2,1024,128]{2,1,0:T(8,128)(2,1)}, u32[]{:S(2)}) copy-start(bf16[2,1024,128]{2,1,0:T(8,128)(2,1)} %param.8) | copy-start | bytes 1572868
  1.3 13.8 %all-to-all-start = ((s32[4,4,16]{2,1,0:T(4,128)}), s32[4,4,16]{2,1,0:T(4,128)S(1)}, u32[]{:S(2)}, u32[]{:S(2)}) async-start(s32[4,4,16]{2,1,0:T(4,128)} %broadcast_in_dim.41), calls=%async_computation | async-start | bytes 16384 | tf_op jit(solution)/shard_map/all_to_all | solution.py:270
  7.7 7.4 %collective-permute-start = (bf16[8,128,128]{2,1,0:T(8,128)(2,1)S(1)}, bf16[8,128,128]{2,1,0:T(8,128)(2,1)S(1)}, u32[]{:S(2)}, u32[]{:S(2)}) collective-permute-start(bf16[8,128,128]{2,1,0:T(8,128)(2,1)S(1)} %bitcast.67), channel_id=1, source_target_pairs={{0,1},{1,2},{2,3},{3,0},{4,5},{5,6},{6,7},{7,4},{8,9},{9,10},{10,1... | collective-permute-start | bytes 786440 | tf_op jit(solution)/shard_map/ppermute | solution.py:37
  7.9 7.1 %copy-start.5 = (bf16[4,1024,128]{2,1,0:T(8,128)(2,1)S(1)}, bf16[4,1024,128]{2,1,0:T(8,128)(2,1)}, u32[]{:S(2)}) copy-start(bf16[4,1024,128]{2,1,0:T(8,128)(2,1)} %param.9) | copy-start | bytes 3145732
  15.8 31.0 %all-to-all-start.1 = ((bf16[4,64,32,128]{3,2,1,0:T(8,128)(2,1)}), bf16[4,64,32,128]{3,2,1,0:T(8,128)(2,1)S(1)}, u32[]{:S(2)}, u32[]{:S(2)}) async-start(bf16[4,64,32,128]{3,2,1,0:T(8,128)(2,1)} %shard_map.82), calls=%async_computation.1 | async-start | bytes 4194304 | tf_op jit(solution)/shard_map/all_to_all | solution.py:270
  21.9 16.4 %collective-permute-start.1 = (s32[4,64]{1,0:T(4,128)S(1)}, s32[4,64]{1,0:T(4,128)S(1)}, u32[]{:S(2)}, u32[]{:S(2)}) collective-permute-start(s32[4,64]{1,0:T(4,128)S(1)} %reshape.151), channel_id=1, source_target_pairs={{0,4},{4,0},{1,5},{5,1},{2,6},{6,2},{3,7},{7,3},{8,12},{12,8},{9,1... | collective-permute-start | bytes 3080 | tf_op jit(solution)/shard_map/ppermute | solution.py:37
  38.2 4.9 %collective-permute-start.4 = (s32[2,16]{1,0:T(2,128)S(1)}, s32[2,16]{1,0:T(2,128)S(1)}, u32[]{:S(2)}, u32[]{:S(2)}) collective-permute-start(s32[2,16]{1,0:T(2,128)S(1)} %bitcast.71), channel_id=1, source_target_pairs={{0,24},{8,0},{16,8},{24,16},{1,25},{9,1},{17,9},{25,17},{2,26},{10... | collective-permute-start | bytes 392 | tf_op jit(solution)/shard_map/ppermute | solution.py:37
  40.7 5.1 %collective-permute-start.3 = (s32[2,16]{1,0:T(2,128)S(1)}, s32[2,16]{1,0:T(2,128)S(1)}, u32[]{:S(2)}, u32[]{:S(2)}) collective-permute-start(s32[2,16]{1,0:T(2,128)S(1)} %bitcast.72), channel_id=1, source_target_pairs={{0,16},{8,24},{16,0},{24,8},{1,17},{9,25},{17,1},{25,9},{2,18},{10... | collective-permute-start | bytes 392 | tf_op jit(solution)/shard_map/ppermute | solution.py:37
  41.3 4.8 %collective-permute-start.2 = (s32[2,16]{1,0:T(2,128)S(1)}, s32[2,16]{1,0:T(2,128)S(1)}, u32[]{:S(2)}, u32[]{:S(2)}) collective-permute-start(s32[2,16]{1,0:T(2,128)S(1)} %bitcast.73), channel_id=1, source_target_pairs={{0,8},{8,16},{16,24},{24,0},{1,9},{9,17},{17,25},{25,1},{2,10},{10... | collective-permute-start | bytes 392 | tf_op jit(solution)/shard_map/ppermute | solution.py:37
  46.9 4.2 %collective-permute-start.5 = (bf16[256,32,128]{2,1,0:T(8,128)(2,1)S(1)}, bf16[256,32,128]{2,1,0:T(8,128)(2,1)S(1)}, u32[]{:S(2)}, u32[]{:S(2)}) collective-permute-start(bf16[256,32,128]{2,1,0:T(8,128)(2,1)S(1)} %bitcast.54), channel_id=1, source_target_pairs={{0,4},{4,0},{1,5},{5,1},{2,6},{6,2},{3,7},{7,3},{8,12},{12,8},{9,1... | collective-permute-start | bytes 6291464 | tf_op jit(solution)/shard_map/ppermute | solution.py:37
  54.9 1.4 copy-start.3
  56.2 7.6 %copy-start.9 = (s32[8,8]{1,0:T(8,128)S(1)}, s32[8,8]{1,0:T(8,128)}, u32[]{:S(2)}) copy-start(s32[8,8]{1,0:T(8,128)} %param.15) | copy-start | bytes 772
  56.2 31.7 %all-to-all-start.2 = ((bf16[256,32,128]{2,1,0:T(8,128)(2,1)}), bf16[256,32,128]{2,1,0:T(8,128)(2,1)}, u32[]{:S(2)}, u32[]{:S(2)}) async-start(bf16[256,32,128]{2,1,0:T(8,128)(2,1)} %copy-done.3), calls=%async_computation.2 | async-start | bytes 4194304 | tf_op jit(solution)/shard_map/all_to_all | solution.py:270
  60.8 38.1 %collective-permute-start.6 = (bf16[64,32,128]{2,1,0:T(8,128)(2,1)}, bf16[64,32,128]{2,1,0:T(8,128)(2,1)}, u32[]{:S(2)}, u32[]{:S(2)}) collective-permute-start(bf16[64,32,128]{2,1,0:T(8,128)(2,1)} %get-tuple-element.51), channel_id=1, source_target_pairs={{0,1},{1,2},{2,3},{3,0},{4,5},{5,6},{6,7},{7,4},{8,9},{9,10},{10,1... | collective-permute-start | bytes 1572872 | tf_op jit(solution)/shard_map/ppermute | solution.py:37
  60.9 38.0 %collective-permute-start.7 = (bf16[64,32,128]{2,1,0:T(8,128)(2,1)}, bf16[64,32,128]{2,1,0:T(8,128)(2,1)}, u32[]{:S(2)}, u32[]{:S(2)}) collective-permute-start(bf16[64,32,128]{2,1,0:T(8,128)(2,1)} %get-tuple-element.52), channel_id=1, source_target_pairs={{0,2},{1,3},{2,0},{3,1},{4,6},{5,7},{6,4},{7,5},{8,10},{9,11},{10,... | collective-permute-start | bytes 1572872 | tf_op jit(solution)/shard_map/ppermute | solution.py:37
  63.8 35.1 %collective-permute-start.8 = (bf16[64,32,128]{2,1,0:T(8,128)(2,1)}, bf16[64,32,128]{2,1,0:T(8,128)(2,1)}, u32[]{:S(2)}, u32[]{:S(2)}) collective-permute-start(bf16[64,32,128]{2,1,0:T(8,128)(2,1)} %get-tuple-element.53), channel_id=1, source_target_pairs={{0,3},{1,0},{2,1},{3,2},{4,7},{5,4},{6,5},{7,6},{8,11},{9,8},{10,9... | collective-permute-start | bytes 1572872 | tf_op jit(solution)/shard_map/ppermute | solution.py:37
  63.8 35.2 %collective-permute-start.9 = (bf16[64,32,128]{2,1,0:T(8,128)(2,1)}, bf16[64,32,128]{2,1,0:T(8,128)(2,1)}, u32[]{:S(2)}, u32[]{:S(2)}) collective-permute-start(bf16[64,32,128]{2,1,0:T(8,128)(2,1)} %get-tuple-element.54.rest_0_), channel_id=1, source_target_pairs={{0,4},{4,0},{1,5},{5,1},{2,6},{6,2},{3,7},{7,3},{8,12},{12,8},{9,1... | collective-permute-start | bytes 1572872 | tf_op jit(solution)/shard_map/ppermute | solution.py:37
  63.9 3.1 %copy-start.7 = (bf16[8,128,128]{2,1,0:T(8,128)(2,1)S(1)}, bf16[8,128,128]{2,1,0:T(8,128)(2,1)}, u32[]{:S(2)}) copy-start(bf16[8,128,128]{2,1,0:T(8,128)(2,1)} %param.14) | copy-start | bytes 786436
  90.5 25.3 %all-to-all-start.3 = ((bf16[64,32,128]{2,1,0:T(8,128)(2,1)}), bf16[64,32,128]{2,1,0:T(8,128)(2,1)S(1)}, u32[]{:S(2)}, u32[]{:S(2)}) async-start(bf16[64,32,128]{2,1,0:T(8,128)(2,1)} %shard_map.85), calls=%async_computation.3 | async-start | bytes 1048576 | tf_op jit(solution)/shard_map/all_to_all | solution.py:270
  99.0 2.2 collective-permute-start.10
  99.1 2.9 %collective-permute-start.11 = (bf16[64,32,128]{2,1,0:T(8,128)(2,1)}, bf16[64,32,128]{2,1,0:T(8,128)(2,1)S(1)}, u32[]{:S(2)}, u32[]{:S(2)}) collective-permute-start(bf16[64,32,128]{2,1,0:T(8,128)(2,1)} %collective-permute-done.7.rest_2_), channel_id=1, source_target_pairs={{0,4},{4,0},{1,5},{5,1},{2,6},{6,2},{3,7},{7,3},{8,12},{12,8},{9,1... | collective-permute-start | bytes 1572872 | tf_op jit(solution)/shard_map/ppermute | solution.py:37
  99.6 3.1 %collective-permute-start.12 = (bf16[64,32,128]{2,1,0:T(8,128)(2,1)}, bf16[64,32,128]{2,1,0:T(8,128)(2,1)S(1)}, u32[]{:S(2)}, u32[]{:S(2)}) collective-permute-start(bf16[64,32,128]{2,1,0:T(8,128)(2,1)} %collective-permute-done.8.rest_3_), channel_id=1, source_target_pairs={{0,4},{4,0},{1,5},{5,1},{2,6},{6,2},{3,7},{7,3},{8,12},{12,8},{9,1... | collective-permute-start | bytes 1572872 | tf_op jit(solution)/shard_map/ppermute | solution.py:37
  116.1 2.0 collective-permute-start.13
  116.2 7.1 %collective-permute-start.14 = (bf16[8,32,128]{2,1,0:T(8,128)(2,1)S(1)}, bf16[8,32,128]{2,1,0:T(8,128)(2,1)S(1)}, u32[]{:S(2)}, u32[]{:S(2)}) collective-permute-start(bf16[8,32,128]{2,1,0:T(8,128)(2,1)S(1)} %get-tuple-element.59.own), channel_id=1, source_target_pairs={{0,4},{4,8},{8,12},{12,16},{16,20},{20,24},{24,28},{28,32},{32,36}... | collective-permute-start | bytes 196616 | tf_op jit(solution)/shard_map/ppermute | solution.py:37
  125.2 1.9 collective-permute-start.15
  125.2 7.1 %collective-permute-start.16 = (bf16[8,32,128]{2,1,0:T(8,128)(2,1)S(1)}, bf16[8,32,128]{2,1,0:T(8,128)(2,1)S(1)}, u32[]{:S(2)}, u32[]{:S(2)}) collective-permute-start(bf16[8,32,128]{2,1,0:T(8,128)(2,1)S(1)} %shard_map.88.own), channel_id=1, source_target_pairs={{0,4},{4,8},{8,12},{12,16},{16,20},{20,24},{24,28},{28,32},{32,36}... | collective-permute-start | bytes 196616 | tf_op jit(solution)/shard_map/ppermute | solution.py:37
  134.2 1.9 collective-permute-start.17
  134.2 7.1 %collective-permute-start.18 = (bf16[8,32,128]{2,1,0:T(8,128)(2,1)S(1)}, bf16[8,32,128]{2,1,0:T(8,128)(2,1)S(1)}, u32[]{:S(2)}, u32[]{:S(2)}) collective-permute-start(bf16[8,32,128]{2,1,0:T(8,128)(2,1)S(1)} %shard_map.89.own), channel_id=1, source_target_pairs={{0,4},{4,8},{8,12},{12,16},{16,20},{20,24},{24,28},{28,32},{32,36}... | collective-permute-start | bytes 196616 | tf_op jit(solution)/shard_map/ppermute | solution.py:37
  143.2 13.1 %copy-start.4 = (s32[4,1,16,4]{2,3,1,0:T(4,128)S(1)}, s32[4,1,16,4]{2,3,1,0:T(4,128)}, u32[]{:S(2)}) copy-start(s32[4,1,16,4]{2,3,1,0:T(4,128)} %param.11) | copy-start | bytes 3076
  143.2 26.5 %all-to-all-start.4 = ((bf16[256,32,128]{2,1,0:T(8,128)(2,1)}), bf16[256,32,128]{2,1,0:T(8,128)(2,1)}, u32[]{:S(2)}, u32[]{:S(2)}) async-start(bf16[256,32,128]{2,1,0:T(8,128)(2,1)} %copy-done.2), calls=%async_computation.4 | async-start | bytes 4194304 | tf_op jit(solution)/shard_map/all_to_all | solution.py:270
  147.8 4.3 %collective-permute-start.19 = (bf16[8,32,128]{2,1,0:T(8,128)(2,1)S(1)}, bf16[8,32,128]{2,1,0:T(8,128)(2,1)S(1)}, u32[]{:S(2)}, u32[]{:S(2)}) collective-permute-start(bf16[8,32,128]{2,1,0:T(8,128)(2,1)S(1)} %shard_map.90.rest_0_.refs_0_), channel_id=1, source_target_pairs={{0,1},{1,2},{2,3},{3,0},{4,5},{5,6},{6,7},{7,4},{8,9},{9,10},{10,1... | collective-permute-start | bytes 196616 | tf_op jit(solution)/shard_map/ppermute | solution.py:37
  147.9 5.9 %collective-permute-start.20 = (bf16[8,32,128]{2,1,0:T(8,128)(2,1)S(1)}, bf16[8,32,128]{2,1,0:T(8,128)(2,1)S(1)}, u32[]{:S(2)}, u32[]{:S(2)}) collective-permute-start(bf16[8,32,128]{2,1,0:T(8,128)(2,1)S(1)} %shard_map.90.rest_0_.refs_0_), channel_id=1, source_target_pairs={{0,2},{1,3},{2,0},{3,1},{4,6},{5,7},{6,4},{7,5},{8,10},{9,11},{10,... | collective-permute-start | bytes 196616 | tf_op jit(solution)/shard_map/ppermute | solution.py:37
  150.8 5.5 %collective-permute-start.21 = (bf16[8,32,128]{2,1,0:T(8,128)(2,1)S(1)}, bf16[8,32,128]{2,1,0:T(8,128)(2,1)S(1)}, u32[]{:S(2)}, u32[]{:S(2)}) collective-permute-start(bf16[8,32,128]{2,1,0:T(8,128)(2,1)S(1)} %shard_map.90.rest_0_.refs_0_), channel_id=1, source_target_pairs={{0,3},{1,0},{2,1},{3,2},{4,7},{5,4},{6,5},{7,6},{8,11},{9,8},{10,9... | collective-permute-start | bytes 196616 | tf_op jit(solution)/shard_map/ppermute | solution.py:37
  156.3 1.6 copy-start.1
  159.9 5.2 %collective-permute-start.22 = (bf16[16,32,128]{2,1,0:T(8,128)(2,1)}, bf16[16,32,128]{2,1,0:T(8,128)(2,1)S(1)}, u32[]{:S(2)}, u32[]{:S(2)}) collective-permute-start(bf16[16,32,128]{2,1,0:T(8,128)(2,1)} %get-tuple-element.63), channel_id=1, source_target_pairs={{0,1},{1,2},{2,3},{3,0},{4,5},{5,6},{6,7},{7,4},{8,9},{9,10},{10,1... | collective-permute-start | bytes 393224 | tf_op jit(solution)/shard_map/ppermute | solution.py:37
  160.5 6.9 %collective-permute-start.23 = (bf16[16,32,128]{2,1,0:T(8,128)(2,1)}, bf16[16,32,128]{2,1,0:T(8,128)(2,1)}, u32[]{:S(2)}, u32[]{:S(2)}) collective-permute-start(bf16[16,32,128]{2,1,0:T(8,128)(2,1)} %get-tuple-element.64), channel_id=1, source_target_pairs={{0,2},{1,3},{2,0},{3,1},{4,6},{5,7},{6,4},{7,5},{8,10},{9,11},{10,... | collective-permute-start | bytes 393224 | tf_op jit(solution)/shard_map/ppermute | solution.py:37
  161.5 7.2 %collective-permute-start.24 = (bf16[16,32,128]{2,1,0:T(8,128)(2,1)}, bf16[16,32,128]{2,1,0:T(8,128)(2,1)}, u32[]{:S(2)}, u32[]{:S(2)}) collective-permute-start(bf16[16,32,128]{2,1,0:T(8,128)(2,1)} %get-tuple-element.65), channel_id=1, source_target_pairs={{0,3},{1,0},{2,1},{3,2},{4,7},{5,4},{6,5},{7,6},{8,11},{9,8},{10,9... | collective-permute-start | bytes 393224 | tf_op jit(solution)/shard_map/ppermute | solution.py:37
  165.1 3.6 %copy-start.8 = (bf16[16,32,128]{2,1,0:T(8,128)(2,1)}, bf16[16,32,128]{2,1,0:T(8,128)(2,1)S(1)}, u32[]{:S(2)}) copy-start(bf16[16,32,128]{2,1,0:T(8,128)(2,1)S(1)} %collective-permute-done.22) | copy-start | bytes 393220
  182.3 1.9 collective-permute-start.25
  208.5 2.0 collective-permute-start.26
  208.6 7.1 %collective-permute-start.27 = (bf16[8,32,128]{2,1,0:T(8,128)(2,1)S(1)}, bf16[8,32,128]{2,1,0:T(8,128)(2,1)S(1)}, u32[]{:S(2)}, u32[]{:S(2)}) collective-permute-start(bf16[8,32,128]{2,1,0:T(8,128)(2,1)S(1)} %get-tuple-element.67.own), channel_id=1, source_target_pairs={{0,4},{4,8},{8,12},{12,16},{16,20},{20,24},{24,28},{28,32},{32,36}... | collective-permute-start | bytes 196616 | tf_op jit(solution)/shard_map/ppermute | solution.py:37
  217.6 1.9 collective-permute-start.28
  217.6 7.1 %collective-permute-start.29 = (bf16[8,32,128]{2,1,0:T(8,128)(2,1)S(1)}, bf16[8,32,128]{2,1,0:T(8,128)(2,1)S(1)}, u32[]{:S(2)}, u32[]{:S(2)}) collective-permute-start(bf16[8,32,128]{2,1,0:T(8,128)(2,1)S(1)} %shard_map.94.own), channel_id=1, source_target_pairs={{0,4},{4,8},{8,12},{12,16},{16,20},{20,24},{24,28},{28,32},{32,36}... | collective-permute-start | bytes 196616 | tf_op jit(solution)/shard_map/ppermute | solution.py:37
  226.6 1.9 collective-permute-start.30
  226.6 7.1 %collective-permute-start.31 = (bf16[8,32,128]{2,1,0:T(8,128)(2,1)S(1)}, bf16[8,32,128]{2,1,0:T(8,128)(2,1)S(1)}, u32[]{:S(2)}, u32[]{:S(2)}) collective-permute-start(bf16[8,32,128]{2,1,0:T(8,128)(2,1)S(1)} %shard_map.95.own), channel_id=1, source_target_pairs={{0,4},{4,8},{8,12},{12,16},{16,20},{20,24},{24,28},{28,32},{32,36}... | collective-permute-start | bytes 196616 | tf_op jit(solution)/shard_map/ppermute | solution.py:37
  235.6 4.3 %collective-permute-start.32 = (bf16[8,32,128]{2,1,0:T(8,128)(2,1)S(1)}, bf16[8,32,128]{2,1,0:T(8,128)(2,1)S(1)}, u32[]{:S(2)}, u32[]{:S(2)}) collective-permute-start(bf16[8,32,128]{2,1,0:T(8,128)(2,1)S(1)} %shard_map.96.refs_4_), channel_id=1, source_target_pairs={{0,1},{1,2},{2,3},{3,0},{4,5},{5,6},{6,7},{7,4},{8,9},{9,10},{10,1... | collective-permute-start | bytes 196616 | tf_op jit(solution)/shard_map/ppermute | solution.py:37
  236.4 5.8 %collective-permute-start.33 = (bf16[8,32,128]{2,1,0:T(8,128)(2,1)S(1)}, bf16[8,32,128]{2,1,0:T(8,128)(2,1)S(1)}, u32[]{:S(2)}, u32[]{:S(2)}) collective-permute-start(bf16[8,32,128]{2,1,0:T(8,128)(2,1)S(1)} %shard_map.96.refs_4_), channel_id=1, source_target_pairs={{0,2},{1,3},{2,0},{3,1},{4,6},{5,7},{6,4},{7,5},{8,10},{9,11},{10,... | collective-permute-start | bytes 196616 | tf_op jit(solution)/shard_map/ppermute | solution.py:37
  238.6 5.5 %collective-permute-start.34 = (bf16[8,32,128]{2,1,0:T(8,128)(2,1)S(1)}, bf16[8,32,128]{2,1,0:T(8,128)(2,1)S(1)}, u32[]{:S(2)}, u32[]{:S(2)}) collective-permute-start(bf16[8,32,128]{2,1,0:T(8,128)(2,1)S(1)} %shard_map.96.refs_4_), channel_id=1, source_target_pairs={{0,3},{1,0},{2,1},{3,2},{4,7},{5,4},{6,5},{7,6},{8,11},{9,8},{10,9... | collective-permute-start | bytes 196616 | tf_op jit(solution)/shard_map/ppermute | solution.py:37
  (2 other events, 2.1 us)
